TPU v7x, 32 devices: a whole 2x2x4 slice. The times are simulated.
32 devices in a mesh: dp: 2 (over core), space: 16 (over z, y, x).
Axes of the slice: x: 2, y: 2, z: 4, core: 2. Of those that a mesh axis runs over, the one named last changes fastest.
Arguments:
- features: bfloat16 [2, 1024, 16, 1024], P('dp', 'space'), may hold values from -6 to 6
- psi: bfloat16 [2, 1024, 64, 256], P('dp', 'space'), may hold values from -0.75 to 0.75
- neighbors: int32 [2, 1024, 16], P('dp', 'space'), may hold values from 0 to 1023, as said below
- counts: int32 [2, 1024], P('dp', 'space'), may hold values from 4 to 16, as said below
- occupation: float32 [2, 256], P('dp'), may hold values from 0.1 to 1
- weights: bfloat16 [1024, 4096], P(None, 'space'), may hold values from -0.1875 to 0.1875
Outputs:
- energies: float32 [2, 256], P('dp')
- gradient: float32 [4096, 1024], P('space')
Inputs may be any that keep to these rules, and one draw needn't show every extreme that they name: `neighbors`: every neighbor tile lies in the same cluster of 64 consecutive tiles or in one of the two clusters beside it, counted around a closed loop of 16 clusters. `counts`: the first tile of every twist uses all 16 slots.
All inputs are finite; a program needn't handle non-finite values.
Results may differ from a plain program's by a relative error of at most 0.004.
Values may be sent and summed in bfloat16 or wider, within the bound.
A program may use at most 192 MiB of HBM per device.

v0:
```python
import math

import jax
import jax.numpy as jnp
from jax import lax
from jax.sharding import PartitionSpec as P


def with_halo(value, sides, width):
    for axis, dim in sides:
        size, length = (lax.axis_size(axis), value.shape[dim])
        up = [(i, (i + 1) % size) for i in range(size)]
        down = [(j, i) for i, j in up]
        last = lax.slice_in_dim(value, length - width, length, axis=dim)
        leading = lax.slice_in_dim(value, 0, width, axis=dim)
        before = lax.ppermute(last, axis, up)
        after = lax.ppermute(leading, axis, down)
        value = jnp.concatenate([before, value, after], axis=dim)
    return value


def local(features, psi, neighbors, counts, occupation, weights):
    twists_here, rows, slots, width = features.shape
    orbit = psi.shape[2]
    bands = psi.shape[3]
    nspace = lax.axis_size("space")
    myself = lax.axis_index("space")
    factor = 1.0 / math.sqrt(rows * nspace * slots)
    flat = features.reshape(twists_here * rows * slots, width)
    products = jnp.dot(
        flat,
        lax.all_gather(weights, "space", axis=1, tiled=True),
        preferred_element_type=jnp.float32,
    )
    valid = (
        lax.broadcasted_iota(jnp.int32, (twists_here, rows, slots), 2) < counts[:, :, None]
    ).astype(jnp.bfloat16)
    blocks = (
        products.astype(jnp.bfloat16).reshape(twists_here, rows, slots, orbit, orbit)
        * valid[:, :, :, None, None]
    )
    widened = with_halo(psi, (("space", 1),), rows)
    owners = neighbors // rows
    placed = (owners - myself + 1 + nspace) % nspace * rows + neighbors % rows
    weighted = (psi.astype(jnp.float32) * occupation[:, None, None, :]).astype(jnp.bfloat16)

    def per_slot(carry, inputs):
        block_k, index_k, valid_k = inputs
        fetched = jax.vmap(lambda table, where: table[where])(widened, index_k)
        carry = carry + jnp.einsum(
            "trac,trcb->trab", block_k, fetched, preferred_element_type=jnp.float32
        )
        grad_k = (
            factor
            * jnp.einsum("trab,trcb->trac", weighted, fetched, preferred_element_type=jnp.float32)
        ).astype(jnp.bfloat16)
        return (carry, grad_k * valid_k[:, :, None, None])

    inputs = (jnp.moveaxis(blocks, 2, 0), jnp.moveaxis(placed, 2, 0), jnp.moveaxis(valid, 2, 0))
    applied, dblocks = lax.scan(
        per_slot, jnp.zeros((twists_here, rows, orbit, bands), jnp.float32), inputs
    )
    partial_energy = factor * jnp.sum(psi.astype(jnp.float32) * applied, axis=(1, 2))
    energies = lax.psum(partial_energy, "space")
    square = orbit * orbit
    flat_grads = dblocks.reshape(slots, twists_here, rows, square)
    share = lax.psum_scatter(
        jnp.einsum("strO,trsf->Of", flat_grads, features, preferred_element_type=jnp.float32),
        "space",
        scatter_dimension=0,
        tiled=True,
    )
    gradient = lax.psum(share, "dp")
    return (energies, gradient)


def solution(mesh):
    placed = (
        P("dp", "space", None, None),
        P("dp", "space", None, None),
        P("dp", "space", None),
        P("dp", "space"),
        P("dp", None),
        P(None, "space"),
    )
    return jax.shard_map(
        local,
        mesh=mesh,
        in_specs=placed,
        out_specs=(P("dp", None), P("space", None)),
        check_vma=False,
    )
```

profile of v0, /device:TPU:0, one launch (start us, length us, event | category | flops | bytes accessed | tf_op | source)
XLA Modules:
  0.0 968.4 jit_solution(7264657905399007959)
XLA Ops:
  8.0 3.0 collective-permute-start
  10.9 4.1 collective-permute-start.1
  17.3 3.5 fusion.16
  20.8 97.2 %collective-permute-done = bf16[1,64,64,256]{3,2,1,0:T(8,128)(2,1)} collective-permute-done((bf16[1,64,64,256]{3,2,1,0:T(8,128)(2,1)}, bf16[1,64,64,256]{3,2,1,0:T(8,128)(2,1)}, u32[]{:S(2)}, u32[]{:S(2)}) %collective-permute-start) | collective-permute-done | bytes 2097184 | tf_op jit(solution)/shard_map/ppermute | solution.py:16
  119.9 5.5 pad_maximum_fusion
  125.4 77.2 %all-gather.2.cloned.1.call-done = bf16[1024,4096]{1,0:T(8,128)(2,1)} async-done(((bf16[1024,256]{1,0:T(8,128)(2,1)}), bf16[1024,4096]{1,0:T(8,128)(2,1)}) %all-gather.2.cloned.1.call-update) | async-done | bytes 8388624 | tf_op jit(solution)/shard_map/all_gather | solution.py:32
  202.6 14.2 %convolution_convert_fusion = bf16[1024,4096]{1,0:T(8,128)(2,1)} fusion(bf16[1024,1024]{1,0:T(8,128)(2,1)S(1)} %bitcast.74, bf16[1024,4096]{1,0:T(8,128)(2,1)} %all-gather.2.cloned.1.call-done), kind=kOutput, calls=%fused_computation.21 | convolution fusion | flops 8594128896 | bytes 18874368 | tf_op jit(solution)/shard_map/dot_general | solution.py:30
  216.8 23.6 %reshape.163 = bf16[1,64,16,64,64]{4,3,2,1,0:T(8,128)(2,1)} reshape(bf16[1024,4096]{1,0:T(8,128)(2,1)} %convolution_convert_fusion) | data formatting | bytes 16777216 | tf_op jit(solution)/shard_map/reshape | solution.py:39
  240.4 14.0 %fusion.15 = bf16[16,1,64,64,64]{4,3,2,1,0:T(8,128)(2,1)} fusion(bf16[1,64,16,64,64]{4,3,2,1,0:T(8,128)(2,1)} %reshape.163, bf16[64,16]{0,1:T(8,128)(2,1)S(1)} %fusion.24), kind=kLoop, calls=%fused_computation.19 | loop fusion | flops 4194304 | bytes 16779264 | tf_op jit(solution)/shard_map/transpose | solution.py:59
  254.4 274.0 %while.13 = (s32[]{:T(128)}, f32[1,64,64,256]{3,2,1,0:T(8,128)}, bf16[16,1,64,64,64]{4,3,2,0,1:T(8,128)(2,1)}, bf16[16,1,64,64,64]{4,3,2,1,0:T(8,128)(2,1)}, s32...) while((s32[]{:T(128)}, f32[1,64,64,256]{3,2,1,0:T(8,128)}, ...), condition=%wide.region_1.2_spmd.clone, body=%wide.region_0.1_spmd.clone.sunk | while | flops 271319552 | bytes 23071752 | solution.py:60
  254.4 4.8 gather_fusion
  259.2 3.9 fusion.41
  264.7 4.6 bitcast_add_fusion.2
  270.4 4.8 gather_fusion
  275.2 3.9 fusion.41
  280.7 5.8 bitcast_add_fusion.2
  287.6 4.8 gather_fusion
  292.4 3.9 fusion.41
  297.9 5.8 bitcast_add_fusion.2
  304.8 4.8 gather_fusion
  309.6 3.9 fusion.41
  315.1 5.8 bitcast_add_fusion.2
  322.0 4.8 gather_fusion
  326.8 3.9 fusion.41
  332.3 5.8 bitcast_add_fusion.2
  339.2 4.8 gather_fusion
  344.0 3.9 fusion.41
  349.5 5.8 bitcast_add_fusion.2
  356.4 4.8 gather_fusion
  361.2 3.9 fusion.41
  366.7 5.8 bitcast_add_fusion.2
  373.6 4.8 gather_fusion
  378.4 3.9 fusion.41
  383.9 5.8 bitcast_add_fusion.2
  390.8 4.8 gather_fusion
  395.6 3.9 fusion.41
  401.1 5.8 bitcast_add_fusion.2
  408.0 4.8 gather_fusion
  412.8 3.9 fusion.41
  418.3 5.8 bitcast_add_fusion.2
  425.2 4.8 gather_fusion
  430.0 3.9 fusion.41
  435.5 5.8 bitcast_add_fusion.2
  442.4 4.8 gather_fusion
  447.2 3.9 fusion.41
  452.7 5.8 bitcast_add_fusion.2
  459.6 4.8 gather_fusion
  464.3 3.9 fusion.41
  469.8 5.8 bitcast_add_fusion.2
  476.8 4.8 gather_fusion
  481.6 3.9 fusion.41
  487.1 5.8 bitcast_add_fusion.2
  494.0 4.8 gather_fusion
  498.8 3.9 fusion.41
  504.3 5.8 bitcast_add_fusion.2
  511.2 4.8 gather_fusion
  516.0 3.9 fusion.41
  521.5 5.8 bitcast_add_fusion.2
  528.4 22.6 %reshape.164 = bf16[16,64,4096]{2,1,0:T(8,128)(2,1)} reshape(bf16[16,1,64,64,64]{4,3,2,0,1:T(8,128)(2,1)} %get-tuple-element.46) | data formatting | bytes 16777216 | tf_op jit(solution)/shard_map/reshape.16
  550.9 15.7 %convolution_bitcast_fusion = f32[4096,1024]{1,0:T(8,128)} fusion(bf16[16,64,4096]{2,1,0:T(8,128)(2,1)} %reshape.164, bf16[64,16,1024]{2,1,0:T(8,128)(2,1)S(1)} %bitcast.75), kind=kOutput, calls=%fused_computation.20 | convolution fusion | flops 8589934592 | bytes 27262976 | tf_op jit(solution)/shard_map/strO,trsf->Of/dot_general | solution.py:68
  566.7 344.7 %reduce-scatter.2.cloned.1.call-done = f32[256,1024]{1,0:T(8,128)} async-done(((f32[4096,1024]{1,0:T(8,128)}), f32[256,1024]{1,0:T(8,128)}) %reduce-scatter.2.cloned.1.call-update) | async-done | bytes 1048592 | tf_op jit(solution)/shard_map/reduce_scatter | solution.py:67
  911.4 3.5 fusion.17
  914.8 44.7 %psum.14 = f32[1,256]{1,0:T(1,128)} all-reduce(f32[1,256]{1,0:T(1,128)S(1)} %bitcast.77), channel_id=1, replica_groups=mesh['dp'=2,'space'=16] {'space'}, use_global_device_ids=true, to_apply=%region_3.4 | all-reduce | flops 256 | bytes 2048 | tf_op jit(solution)/shard_map/psum | solution.py:64
  959.6 2.3 copy.41
  (114 shorter events, 48.2 us)
Async XLA Ops:
  7.2 195.5 %copy-start = (bf16[1,64,16,1024]{3,2,1,0:T(8,128)(2,1)S(1)}, bf16[1,64,16,1024]{3,2,1,0:T(8,128)(2,1)}, u32[]{:S(2)}) copy-start(bf16[1,64,16,1024]{3,2,1,0:T(8,128)(2,1)} %param.8) | copy-start | bytes 6291460
  7.2 195.5 %all-gather.2.cloned.1.call-start = ((), (), s32[]{:S(2)}) async-start(), calls=%async_computation.1 | async-start | bytes 8912896 | tf_op jit(solution)/shard_map/all_gather | solution.py:32
  7.9 903.4 %reduce-scatter.2.cloned.1.call-start = ((), (), s32[]{:S(2)}) async-start(), calls=%async_computation.2 | async-start | bytes 17825792 | tf_op jit(solution)/shard_map/reduce_scatter | solution.py:67
  8.0 110.0 %collective-permute-start = (bf16[1,64,64,256]{3,2,1,0:T(8,128)(2,1)}, bf16[1,64,64,256]{3,2,1,0:T(8,128)(2,1)}, u32[]{:S(2)}, u32[]{:S(2)}) collective-permute-start(bf16[1,64,64,256]{3,2,1,0:T(8,128)(2,1)} %param.9), channel_id=1, source_target_pairs={{0,1},{1,2},{2,3},{3,4},{4,5},{5,6},{6,7},{7,8},{8,9},{9,10},{10,1... | collective-permute-start | bytes 6291464 | tf_op jit(solution)/shard_map/ppermute | solution.py:16
  10.9 108.9 %collective-permute-start.1 = (bf16[1,64,64,256]{3,2,1,0:T(8,128)(2,1)}, bf16[1,64,64,256]{3,2,1,0:T(8,128)(2,1)}, u32[]{:S(2)}, u32[]{:S(2)}) collective-permute-start(bf16[1,64,64,256]{3,2,1,0:T(8,128)(2,1)} %param.9), channel_id=1, source_target_pairs={{1,0},{2,1},{3,2},{4,3},{5,4},{6,5},{7,6},{8,7},{9,8},{10,9},{11,1... | collective-permute-start | bytes 6291464 | tf_op jit(solution)/shard_map/ppermute | solution.py:17
  15.0 104.9 %copy-start.1 = (bf16[1,64,64,256]{3,2,1,0:T(8,128)(2,1)S(1)}, bf16[1,64,64,256]{3,2,1,0:T(8,128)(2,1)}, u32[]{:S(2)}) copy-start(bf16[1,64,64,256]{3,2,1,0:T(8,128)(2,1)} %param.9) | copy-start | bytes 6291460
  566.6 393.0 %all-reduce.2.cloned.1.call-start = ((), (), s32[]{:S(2)}) async-start(), calls=%async_computation.3 | async-start | bytes 2097152 | tf_op jit(solution)/shard_map/psum | solution.py:73
Sparse Core Ops, SparseCore 0:
  10.7 191.8 all-gather.1
  566.7 344.5 reduce-scatter.1
  913.7 25.2 all-reduce.1
where the time goes:
time: 971 us; the launch traced here: 968 us
  waiting for transfers between devices  522 us (54%)
  matrix products  184 us (19%)
  local copies, waits for them, and re-layouts  168 us (17%)
  blocking collectives  44.7 us (5%)
  other arithmetic  28.9 us (3%)
  between operations  13.8 us (1%)
    reduce_scatter x1, waiting for transfers between devices, local(): lax.psum_scatter(jnp.einsum('strO,trsf->Of', flat_grads, features, prefer...  345 us
    ppermute x1, waiting for transfers between devices, with_halo(): before = lax.ppermute(last, axis, up)  97.2 us
    dot_general x16, matrix products, per_slot(): jnp.einsum('trac,trcb->trab', block_k, fetched, preferred_element_type=jn...  92 us
    all_gather x1, waiting for transfers between devices, local(): lax.all_gather(weights, 'space', axis=1, tiled=True)  77.2 us
    gather x32, local copies, waits for them, and re-layouts, per_slot(): fetched = jax.vmap(lambda table, where: table[where])(widened, index_k)  76.5 us
    dot_general x16, matrix products, per_slot(): jnp.einsum('trab,trcb->trac', weighted, fetched, preferred_element_type=j...  62.2 us
    psum x1, blocking collectives, local(): energies = lax.psum(partial_energy, 'space')  44.7 us
    dynamic_update_slice x32, local copies, waits for them, and re-layouts, local(): lax.scan(per_slot, jnp.zeros((twists_here, rows, orbit, bands), jnp.float...  42.7 us
  transfers between devices with their start and end apart: 5, of which 4 were waited for; matrix products, arithmetic and copies ran while one was open for 2% of the time, Pallas kernels for 0%

commit v1 on v0

v1 whole, which is shorter than its diff:
```python
import functools
import math

import jax
import jax.numpy as jnp
from jax import lax
from jax.experimental import pallas as pl
from jax.experimental.pallas import tpu as pltpu
from jax.sharding import PartitionSpec as P

GROUP = 4
PITCH = 40


def with_halo(value, axis, dim):
    size = lax.axis_size(axis)
    up = [(i, (i + 1) % size) for i in range(size)]
    down = [(j, i) for i, j in up]
    before = lax.ppermute(value, axis, up)
    after = lax.ppermute(value, axis, down)
    return jnp.concatenate([before, value, after], axis=dim)


def tile_kernel(
    group, slots, orbit, factor, where_ref, count_ref, h_ref, table_ref, own_ref, occ_ref, d_ref, energy_ref, spread, back, acc
):
    step = pl.program_id(0)
    half = orbit // 2
    lanes = 2 * orbit

    @pl.when(step == 0)
    def _():
        acc[...] = jnp.zeros_like(acc)

    low = lax.broadcasted_iota(jnp.int32, (half, 2 * lanes), 1) % lanes < orbit
    slot = lax.broadcasted_iota(jnp.int32, (slots, 1), 0)
    occ = occ_ref[...]
    total = jnp.zeros(acc.shape, jnp.float32)
    for t in range(group):
        tile = step * group + t
        used = slot < count_ref[tile]
        for q in range(half):
            column = h_ref[t * slots : (t + 1) * slots, q * lanes : (q + 1) * lanes].astype(jnp.float32)
            spread[t, pl.ds(q, slots, stride=PITCH), :] = jnp.where(used, column, 0.0)
        own = own_ref[t * orbit : (t + 1) * orbit, :].astype(jnp.float32)
        weighted = (own * occ).astype(jnp.bfloat16)
        applied = jnp.zeros(acc.shape, jnp.float32)
        for k in range(0, slots, 2):
            block = jnp.concatenate(
                [spread[t, j * PITCH : j * PITCH + half, :] for j in (k, k + 1)], axis=1
            )
            left = jnp.concatenate([jnp.where(low, block, 0.0), jnp.where(low, 0.0, block)], axis=0)
            fetched = [
                table_ref[pl.ds(pl.multiple_of(where_ref[tile * slots + j] * orbit, orbit), orbit), :]
                for j in (k, k + 1)
            ]
            right = jnp.concatenate([fetched[0], fetched[0], fetched[1], fetched[1]], axis=0)
            applied = applied + jnp.dot(left.astype(jnp.bfloat16), right, preferred_element_type=jnp.float32)
            both = lax.dot_general(
                weighted, right, (((1,), (1,)), ((), ())), preferred_element_type=jnp.float32
            )
            chosen = jnp.where(low, both[:half], both[half:]) * factor
            for n, j in enumerate((k, k + 1)):
                back[t, j * PITCH : j * PITCH + half, :] = chosen[:, n * lanes : (n + 1) * lanes]
        total = total + own * applied
        for q in range(half):
            column = back[t, pl.ds(q, slots, stride=PITCH), :]
            d_ref[t * slots : (t + 1) * slots, q * lanes : (q + 1) * lanes] = jnp.where(
                used, column, 0.0
            ).astype(jnp.bfloat16)
    acc[...] += total

    @pl.when(step == pl.num_programs(0) - 1)
    def _():
        energy_ref[...] = factor * jnp.sum(acc[...], axis=0, keepdims=True)


def tiles(blocks, table, own, occupation, where, counts, slots, orbit, factor):
    count = counts.shape[0]
    bands = table.shape[1]
    group = GROUP
    rows, square = blocks.shape
    flops = 2 * rows * square * bands * 4
    return pl.pallas_call(
        functools.partial(tile_kernel, group, slots, orbit, factor),
        out_shape=(
            jax.ShapeDtypeStruct((rows, square), jnp.bfloat16),
            jax.ShapeDtypeStruct((1, bands), jnp.float32),
        ),
        grid_spec=pltpu.PrefetchScalarGridSpec(
            num_scalar_prefetch=2,
            grid=(count // group,),
            in_specs=[
                pl.BlockSpec((group * slots, square), lambda i, *_: (i, 0)),
                pl.BlockSpec(table.shape, lambda i, *_: (0, 0), pipeline_mode=pl.Buffered(1)),
                pl.BlockSpec((group * orbit, bands), lambda i, *_: (i, 0)),
                pl.BlockSpec((1, bands), lambda i, *_: (0, 0)),
            ],
            out_specs=[
                pl.BlockSpec((group * slots, square), lambda i, *_: (i, 0)),
                pl.BlockSpec((1, bands), lambda i, *_: (0, 0)),
            ],
            scratch_shapes=[
                pltpu.VMEM((group, slots * PITCH, 2 * orbit), jnp.float32),
                pltpu.VMEM((group, slots * PITCH, 2 * orbit), jnp.float32),
                pltpu.VMEM((orbit, bands), jnp.float32),
            ],
        ),
        compiler_params=pltpu.CompilerParams(vmem_limit_bytes=40 * 2**20),
        cost_estimate=pl.CostEstimate(flops=flops, bytes_accessed=4 * rows * square, transcendentals=0),
    )(where, counts, blocks, table, own, occupation)


def local(features, psi, neighbors, counts, occupation, weights):
    _, rows, slots, width = features.shape
    orbit, bands = psi.shape[2:]
    nspace = lax.axis_size("space")
    myself = lax.axis_index("space")
    factor = 1.0 / math.sqrt(rows * nspace * slots)
    flat = features.reshape(rows * slots, width)
    own = psi.reshape(rows, orbit // 2, 2, bands).swapaxes(1, 2).reshape(rows * orbit, bands)
    table = with_halo(psi.reshape(rows * orbit, bands), "space", 0)
    where = (neighbors // rows - myself + 1 + nspace) % nspace * rows + neighbors % rows
    blocks = jnp.dot(
        flat, lax.all_gather(weights, "space", axis=1, tiled=True), preferred_element_type=jnp.float32
    ).astype(jnp.bfloat16)
    dblocks, energy = tiles(
        blocks, table, own, occupation, where.reshape(-1), counts.reshape(-1), slots, orbit, factor
    )
    energies = lax.psum(energy, "space")
    partial = lax.dot_general(dblocks, flat, (((0,), (0,)), ((), ())), preferred_element_type=jnp.float32)
    share = lax.psum_scatter(partial, "space", scatter_dimension=0, tiled=True)
    gradient = lax.psum(share, "dp")
    return (energies, gradient)


def solution(mesh):
    placed = (
        P("dp", "space", None, None),
        P("dp", "space", None, None),
        P("dp", "space", None),
        P("dp", "space"),
        P("dp", None),
        P(None, "space"),
    )
    return jax.shard_map(
        local,
        mesh=mesh,
        in_specs=placed,
        out_specs=(P("dp", None), P("space", None)),
        check_vma=False,
    )
```

time: 971 us -> 670 us (0.69)
  local copies, waits for them, and re-layouts: 168 us -> 10.2 us
  matrix products: 184 us -> 28.9 us
  Pallas kernels: 0 us -> 36.1 us
  other arithmetic: 28.9 us -> 9.76 us
    dot_general x33 -> x1, matrix products: 170 us -> 14.6 us  [local(): lax.dot_general(dblocks, flat, (((0,), (0,)), ((), ())), preferred_elemen...]
    gather x32 -> x0, local copies, waits for them, and re-layouts: 76.5 us -> none  [per_slot(): fetched = jax.vmap(lambda table, where: table[where])(widened, index_k)]
    dynamic_update_slice x32 -> x0, local copies, waits for them, and re-layouts: 42.7 us -> none  [local(): lax.scan(per_slot, jnp.zeros((twists_here, rows, orbit, bands), jnp.float...]
    pallas_call x0 -> x1, Pallas kernels: none -> 36.1 us  [tiles(): pl.pallas_call(functools.partial(tile_kernel, group, slots, orbit, factor...]
    another operation x1 -> x0, local copies, waits for them, and re-layouts: 22.6 us -> none
    reshape x1 -> x3, local copies, waits for them, and re-layouts: 23.6 us -> 7.8 us  [the longest x2 7.72 us: local(): psi.reshape(rows, orbit // 2, 2, bands).swapaxes(1, 2)]
    transpose x3 -> x0, other arithmetic: 15.5 us -> none  [the longest x1 14 us: local(): jnp.moveaxis(blocks, 2, 0)]
  transfers between devices with their start and end apart: 5 -> 5, of which waited for: 4 -> 4; matrix products, arithmetic and copies ran while one was open for 2% -> 3% of each run, Pallas kernels for 0% -> 0%
where the time goes in v1:
time: 670 us; the launch traced here: 669 us
  waiting for transfers between devices  519 us (77%)
  blocking collectives  44.7 us (7%)
  Pallas kernels  36.1 us (5%)
  matrix products  28.9 us (4%)
  between operations  13.8 us (2%)
  local copies, waits for them, and re-layouts  10.2 us (2%)
  other arithmetic  9.76 us (1%)
  starting transfers between devices  7.1 us (1%)
    reduce_scatter x1, waiting for transfers between devices, local(): share = lax.psum_scatter(partial, 'space', scatter_dimension=0, tiled=True)  345 us
    all_gather x1, waiting for transfers between devices, local(): lax.all_gather(weights, 'space', axis=1, tiled=True)  77 us
    ppermute x1, waiting for transfers between devices, with_halo(): before = lax.ppermute(value, axis, up)  51.2 us
    ppermute x1, waiting for transfers between devices, with_halo(): after = lax.ppermute(value, axis, down)  45.1 us
    psum x1, blocking collectives, local(): energies = lax.psum(energy, 'space')  44.7 us
    pallas_call x1, Pallas kernels, tiles(): pl.pallas_call(functools.partial(tile_kernel, group, slots, orbit, factor...  36.1 us
    dot_general x1, matrix products, local(): lax.dot_general(dblocks, flat, (((0,), (0,)), ((), ())), preferred_elemen...  14.6 us
    dot_general x1, matrix products, local(): jnp.dot(flat, lax.all_gather(weights, 'space', axis=1, tiled=True), prefe...  14.3 us
  transfers between devices with their start and end apart: 5, of which 4 were waited for; matrix products, arithmetic and copies ran while one was open for 3% of the time, Pallas kernels for 0%

profile of v1, /device:TPU:0, one launch (start us, length us, event | category | flops | bytes accessed | tf_op | source)
XLA Modules:
  0.0 669.3 jit_solution(15238519537639775498)
XLA Ops:
  7.2 0.0 copy-start
  7.2 0.0 all-gather.2.cloned.1.call-start
  7.2 0.7 all-gather.2.cloned.1.call-update
  7.9 0.0 reduce-scatter.2.cloned.1.call-start
  8.0 7.0 %collective-permute-start.1 = (bf16[4096,256]{1,0:T(8,128)(2,1)}, bf16[4096,256]{1,0:T(8,128)(2,1)}, u32[]{:S(2)}, u32[]{:S(2)}) collective-permute-start(bf16[4096,256]{1,0:T(8,128)(2,1)} %bitcast.16), channel_id=1, source_target_pairs={{1,0},{2,1},{3,2},{4,3},{5,4},{6,5},{7,6},{8,7},{9,8},{10,9},{11,1... | collective-permute-start | bytes 6291464 | tf_op jit(solution)/shard_map/ppermute | solution.py:20
  14.9 0.0 collective-permute-start
  14.9 4.2 reshape.26
  19.1 0.7 fusion.4
  19.8 0.1 copy.9
  19.9 0.1 reshape.22.where_ref
  20.0 3.6 copy.10
  23.6 45.1 %collective-permute-done.1 = bf16[4096,256]{1,0:T(8,128)(2,1)} collective-permute-done((bf16[4096,256]{1,0:T(8,128)(2,1)}, bf16[4096,256]{1,0:T(8,128)(2,1)}, u32[]{:S(2)}, u32[]{:S(2)}) %collective-permute-start.1) | collective-permute-done | bytes 2097184 | tf_op jit(solution)/shard_map/ppermute | solution.py:20
  68.6 51.2 %collective-permute-done = bf16[4096,256]{1,0:T(8,128)(2,1)} collective-permute-done((bf16[4096,256]{1,0:T(8,128)(2,1)}, bf16[4096,256]{1,0:T(8,128)(2,1)}, u32[]{:S(2)}, u32[]{:S(2)}) %collective-permute-start) | collective-permute-done | bytes 2097184 | tf_op jit(solution)/shard_map/ppermute | solution.py:19
  119.8 9.0 %pad_maximum_fusion.table_ref = bf16[12288,256]{1,0:T(8,128)(2,1)} fusion(bf16[4096,256]{1,0:T(8,128)(2,1)} %collective-permute-done.1, bf16[4096,256]{1,0:T(8,128)(2,1)} %bitcast.18, bf16[4096,256]{1,0:T(8,128)(2,1)} %collective-permute-done), kind=kLoop, calls=%fused_computation.1 | loop fusion | flops 18874368 | bytes 12582912 | tf_op jit(solution)/shard_map/concatenate | solution.py:21
  128.8 77.0 %all-gather.2.cloned.1.call-done = bf16[1024,4096]{1,0:T(8,128)(2,1)} async-done(((bf16[1024,256]{1,0:T(8,128)(2,1)}), bf16[1024,4096]{1,0:T(8,128)(2,1)}) %all-gather.2.cloned.1.call-update) | async-done | bytes 8388624 | tf_op jit(solution)/shard_map/all_gather | solution.py:125
  205.9 0.0 copy-done
  205.9 0.0 copy-start.1
  205.9 0.0 copy-start.2
  205.9 0.0 copy-start.3
  205.9 0.0 copy-start.4
  205.9 14.3 %convolution_convert_fusion.h_ref = bf16[1024,4096]{1,0:T(8,128)(2,1)} fusion(bf16[1024,1024]{1,0:T(8,128)(2,1)S(1)} %bitcast.12, bf16[1024,4096]{1,0:T(8,128)(2,1)} %all-gather.2.cloned.1.call-done), kind=kOutput, calls=%fused_computation | convolution fusion | flops 8594128896 | bytes 18874368 | tf_op jit(solution)/shard_map/dot_general | solution.py:124
  220.2 0.0 copy-done.1
  220.2 0.0 copy-done.2
  220.2 0.0 copy-done.3
  220.3 0.0 copy-done.4
  220.3 36.1 %shard_map.77 = (bf16[1024,4096]{1,0:T(8,128)(2,1)}, f32[1,256]{1,0:T(1,128)S(1)}) custom-call(s32[1024]{0:T(1024)S(1)} %reshape.22.where_ref, s32[64]{0:T(128)S(1)} %bitcast.15, bf16[1024,4096]{1,0:T(8,128)(2,1)} %convolution_convert_fusion.h_ref, bf16[12288,256]{1,0:T(8,128)(2,1)S(1)} %copy-done.1, bf16[4096,256]{1,0:T(8,128)(2,1)S(1)} %bitcast.14, ...), custom_call_target="tpu_custom_call" | custom-call | flops 8589934592 | bytes 16777216 | tf_op jit(solution)/shard_map/pallas_call | solution.py:84
  256.3 14.6 %fusion.6 = f32[4096,1024]{1,0:T(8,128)} fusion(bf16[1024,4096]{1,0:T(8,128)(2,1)} %get-tuple-element.5, bf16[1024,1024]{1,0:T(8,128)(2,1)S(1)} %bitcast.13), kind=kOutput, calls=%fused_computation.17 | convolution fusion | flops 8589934592 | bytes 27262976 | tf_op jit(solution)/shard_map/dot_general | solution.py:131
  270.9 0.0 reduce-scatter.2.cloned.1.call-update
  270.9 0.0 all-reduce.2.cloned.1.call-start
  271.0 344.7 %reduce-scatter.2.cloned.1.call-done = f32[256,1024]{1,0:T(8,128)} async-done(((f32[4096,1024]{1,0:T(8,128)}), f32[256,1024]{1,0:T(8,128)}) %reduce-scatter.2.cloned.1.call-update) | async-done | bytes 1048592 | tf_op jit(solution)/shard_map/reduce_scatter | solution.py:132
  615.7 0.0 all-reduce.2.cloned.1.call-update
  615.7 44.7 %psum.14 = f32[1,256]{1,0:T(1,128)} all-reduce(f32[1,256]{1,0:T(1,128)S(1)} %get-tuple-element.4), channel_id=1, replica_groups=mesh['dp'=2,'space'=16] {'space'}, use_global_device_ids=true, to_apply=%region_0.1 | all-reduce | flops 256 | bytes 2048 | tf_op jit(solution)/shard_map/psum | solution.py:130
  660.4 0.0 all-reduce.2.cloned.1.call-done
  660.4 2.3 copy.12
Async XLA Ops:
  7.2 198.7 %copy-start = (bf16[1,64,16,1024]{3,2,1,0:T(8,128)(2,1)S(1)}, bf16[1,64,16,1024]{3,2,1,0:T(8,128)(2,1)}, u32[]{:S(2)}) copy-start(bf16[1,64,16,1024]{3,2,1,0:T(8,128)(2,1)} %param.6) | copy-start | bytes 6291460
  7.2 198.7 %all-gather.2.cloned.1.call-start = ((), (), s32[]{:S(2)}) async-start(), calls=%async_computation.1 | async-start | bytes 8912896 | tf_op jit(solution)/shard_map/all_gather | solution.py:125
  7.9 607.7 %reduce-scatter.2.cloned.1.call-start = ((), (), s32[]{:S(2)}) async-start(), calls=%async_computation.2 | async-start | bytes 17825792 | tf_op jit(solution)/shard_map/reduce_scatter | solution.py:132
  8.0 60.7 %collective-permute-start.1 = (bf16[4096,256]{1,0:T(8,128)(2,1)}, bf16[4096,256]{1,0:T(8,128)(2,1)}, u32[]{:S(2)}, u32[]{:S(2)}) collective-permute-start(bf16[4096,256]{1,0:T(8,128)(2,1)} %bitcast.16), channel_id=1, source_target_pairs={{1,0},{2,1},{3,2},{4,3},{5,4},{6,5},{7,6},{8,7},{9,8},{10,9},{11,1... | collective-permute-start | bytes 6291464 | tf_op jit(solution)/shard_map/ppermute | solution.py:20
  14.9 104.9 %collective-permute-start = (bf16[4096,256]{1,0:T(8,128)(2,1)}, bf16[4096,256]{1,0:T(8,128)(2,1)}, u32[]{:S(2)}, u32[]{:S(2)}) collective-permute-start(bf16[4096,256]{1,0:T(8,128)(2,1)} %bitcast.17), channel_id=1, source_target_pairs={{0,1},{1,2},{2,3},{3,4},{4,5},{5,6},{6,7},{7,8},{8,9},{9,10},{10,1... | collective-permute-start | bytes 6291464 | tf_op jit(solution)/shard_map/ppermute | solution.py:19
  205.9 14.4 %copy-start.1 = (bf16[12288,256]{1,0:T(8,128)(2,1)S(1)}, bf16[12288,256]{1,0:T(8,128)(2,1)}, u32[]{:S(2)}) copy-start(bf16[12288,256]{1,0:T(8,128)(2,1)} %pad_maximum_fusion.table_ref) | copy-start | bytes 18874372
  205.9 14.4 %copy-start.2 = (bf16[64,32,2,256]{3,1,2,0:T(8,128)(2,1)S(1)}, bf16[64,32,2,256]{3,1,2,0:T(8,128)(2,1)}, u32[]{:S(2)}) copy-start(bf16[64,32,2,256]{3,1,2,0:T(8,128)(2,1)} %copy.10) | copy-start | bytes 6291460
  205.9 14.4 %copy-start.3 = (f32[1,256]{1,0:T(1,128)S(1)}, f32[1,256]{1,0:T(1,128)}, u32[]{:S(2)}) copy-start(f32[1,256]{1,0:T(1,128)} %occ_ref.1) | copy-start | bytes 3076
  205.9 14.4 %copy-start.4 = (s32[1,64]{1,0:T(1,128)S(1)}, s32[1,64]{1,0:T(1,128)}, u32[]{:S(2)}) copy-start(s32[1,64]{1,0:T(1,128)} %param.9) | copy-start | bytes 772
  270.9 389.5 %all-reduce.2.cloned.1.call-start = ((), (), s32[]{:S(2)}) async-start(), calls=%async_computation.3 | async-start | bytes 2097152 | tf_op jit(solution)/shard_map/psum | solution.py:133
Sparse Core Ops, SparseCore 0:
  10.7 195.1 all-gather.1
  271.0 344.5 reduce-scatter.1
  618.0 25.2 all-reduce.1

commit v2 on v1

--- a/solution.py
+++ b/solution.py
@@ -19,6 +19,60 @@
     before = lax.ppermute(value, axis, up)
     after = lax.ppermute(value, axis, down)
     return jnp.concatenate([before, value, after], axis=dim)
+
+
+def swap(value, axis, bit):
+    size = lax.axis_size(axis)
+    return lax.ppermute(value, axis, [(i, i ^ (1 << bit)) for i in range(size)])
+
+
+def chains(size):
+    bits = list(range(size.bit_length() - 1))
+    other = [bit ^ 1 if bit ^ 1 < len(bits) else bit for bit in bits]
+    return bits, other
+
+
+def pair(mine, theirs, mybit, axis):
+    return jnp.where(mybit == 0, jnp.stack([mine, theirs], axis), jnp.stack([theirs, mine], axis))
+
+
+def gather_rows(shard):
+    size, me, core = lax.axis_size("space"), lax.axis_index("space"), lax.axis_index("dp")
+    rows, width = shard.shape
+    halves = lax.dynamic_index_in_dim(shard.reshape(2, 2, rows // 4, width), core, 0, keepdims=False)
+    parts = []
+    for part, order in enumerate(chains(size)):
+        value, done = halves[part], []
+        for bit in reversed(order):
+            axis = sum(d > bit for d in done)
+            value = pair(value, swap(value, "space", bit), me >> bit & 1, axis)
+            done.append(bit)
+        parts.append(value.reshape(size, rows // 4, width))
+    mine = jnp.stack(parts, 1)
+    return pair(mine, swap(mine, "dp", 0), core, 1).reshape(size * rows, width)
+
+
+def scatter_rows(partial):
+    size, me, core = lax.axis_size("space"), lax.axis_index("space"), lax.axis_index("dp")
+    rows, width = partial.shape[0] // size, partial.shape[1]
+    split = partial.reshape(size, 2, 2, rows // 4, width)
+    pick = lambda value, where, axis: lax.dynamic_index_in_dim(value, where, axis, keepdims=False)
+    parts = []
+    for part, order in enumerate(chains(size)):
+        piece = split[:, :, part]
+        value = pick(piece, core, 1).astype(jnp.float32) + swap(pick(piece, 1 - core, 1), "dp", 0)
+        value = value.reshape((2,) * len(order) + value.shape[1:])
+        left = sorted(order, reverse=True)
+        for bit in order:
+            axis, mybit = left.index(bit), me >> bit & 1
+            sent = pick(value, 1 - mybit, axis)
+            if len(left) > 1:
+                sent = sent.astype(jnp.bfloat16)
+            value = pick(value, mybit, axis) + swap(sent, "space", bit)
+            left.remove(bit)
+        parts.append(value)
+    mine = jnp.stack(parts)
+    return pair(mine, swap(mine, "dp", 0), core, 0).reshape(rows, width)
 
 
 def tile_kernel(
@@ -121,16 +175,15 @@
     own = psi.reshape(rows, orbit // 2, 2, bands).swapaxes(1, 2).reshape(rows * orbit, bands)
     table = with_halo(psi.reshape(rows * orbit, bands), "space", 0)
     where = (neighbors // rows - myself + 1 + nspace) % nspace * rows + neighbors % rows
-    blocks = jnp.dot(
-        flat, lax.all_gather(weights, "space", axis=1, tiled=True), preferred_element_type=jnp.float32
+    blocks = lax.dot_general(
+        flat, gather_rows(weights.T), (((1,), (1,)), ((), ())), preferred_element_type=jnp.float32
     ).astype(jnp.bfloat16)
     dblocks, energy = tiles(
         blocks, table, own, occupation, where.reshape(-1), counts.reshape(-1), slots, orbit, factor
     )
     energies = lax.psum(energy, "space")
     partial = lax.dot_general(dblocks, flat, (((0,), (0,)), ((), ())), preferred_element_type=jnp.float32)
-    share = lax.psum_scatter(partial, "space", scatter_dimension=0, tiled=True)
-    gradient = lax.psum(share, "dp")
+    gradient = scatter_rows(partial.astype(jnp.bfloat16))
     return (energies, gradient)
 
 

time: 670 us -> 386 us (0.58)
  waiting for transfers between devices: 519 us -> 178 us
  other arithmetic: 9.76 us -> 38.1 us
  starting transfers between devices: 7.1 us -> 34.8 us
  local copies, waits for them, and re-layouts: 10.2 us -> 29.1 us
  between operations: 13.8 us -> 1.09 us
    reduce_scatter x1 -> x0, waiting for transfers between devices: 345 us -> none  [local(): share = lax.psum_scatter(partial, 'space', scatter_dimension=0, tiled=True)]
    ppermute x0 -> x20, waiting for transfers between devices: none -> 98.9 us  [swap(): return lax.ppermute(value, axis, [(i, i ^ 1 << bit) for i in range(size)])]
    all_gather x1 -> x0, waiting for transfers between devices: 77 us -> none  [local(): lax.all_gather(weights, 'space', axis=1, tiled=True)]
    ppermute x0 -> x20, starting transfers between devices: none -> 26.2 us  [swap(): return lax.ppermute(value, axis, [(i, i ^ 1 << bit) for i in range(size)])]
    add x0 -> x8, other arithmetic: none -> 12.7 us  [the longest x6 7.07 us: scatter_rows(): value = pick(value, mybit, axis) + swap(sent, 'space', bit)]
    select_n x0 -> x17, other arithmetic: none -> 12.3 us  [pair(): jnp.where(mybit == 0, jnp.stack([mine, theirs], axis), jnp.stack([theirs,...]
    ppermute x1, waiting for transfers between devices: 51.2 us -> 41.2 us  [with_halo(): before = lax.ppermute(value, axis, up)]
    select_n x0 -> x3, local copies, waits for them, and re-layouts: none -> 9.04 us  [pair(): jnp.where(mybit == 0, jnp.stack([mine, theirs], axis), jnp.stack([theirs,...]
  transfers between devices with their start and end apart: 5 -> 22, of which waited for: 4 -> 17; matrix products, arithmetic and copies ran while one was open for 3% -> 9% of each run, Pallas kernels for 0% -> 0%
where the time goes in v2:
time: 386 us
  waiting for transfers between devices  178 us (46%)
  blocking collectives  42.5 us (11%)
  other arithmetic  38.1 us (10%)
  Pallas kernels  36.4 us (9%)
  starting transfers between devices  34.8 us (9%)
  local copies, waits for them, and re-layouts  29.1 us (8%)
  matrix products  25.9 us (7%)
    ppermute x20, waiting for transfers between devices, swap(): return lax.ppermute(value, axis, [(i, i ^ 1 << bit) for i in range(size)])  98.9 us
    psum x1, blocking collectives, local(): energies = lax.psum(energy, 'space')  42.5 us
    ppermute x1, waiting for transfers between devices, with_halo(): before = lax.ppermute(value, axis, up)  41.2 us
    ppermute x1, waiting for transfers between devices, with_halo(): after = lax.ppermute(value, axis, down)  38 us
    pallas_call x1, Pallas kernels, tiles(): pl.pallas_call(functools.partial(tile_kernel, group, slots, orbit, factor...  36.4 us
    ppermute x20, starting transfers between devices, swap(): return lax.ppermute(value, axis, [(i, i ^ 1 << bit) for i in range(size)])  26.2 us
    dot_general x1, matrix products, local(): lax.dot_general(flat, gather_rows(weights.T), (((1,), (1,)), ((), ())), p...  14.5 us
    select_n x17, other arithmetic, pair(): jnp.where(mybit == 0, jnp.stack([mine, theirs], axis), jnp.stack([theirs,...  12.3 us
  transfers between devices with their start and end apart: 22, of which 17 were waited for; matrix products, arithmetic and copies ran while one was open for 9% of the time, Pallas kernels for 0%

profile of v2, /device:TPU:0, one launch (start us, length us, event | category | flops | bytes accessed | tf_op | source)
XLA Modules:
  0.0 385.9 jit_solution(18398637067291992775)
XLA Ops:
  0.7 1.4 copy.24
  2.1 4.1 %collective-permute-start = (bf16[64,1024]{1,0:T(8,128)(2,1)S(1)}, bf16[64,1024]{1,0:T(8,128)(2,1)S(1)}, u32[]{:S(2)}, u32[]{:S(2)}) collective-permute-start(bf16[64,1024]{1,0:T(8,128)(2,1)S(1)} %bitcast.128), channel_id=1, source_target_pairs={{0,8},{1,9},{2,10},{3,11},{4,12},{5,13},{6,14},{7,15},{8,0},{9,1},... | collective-permute-start | bytes 393224 | tf_op jit(solution)/shard_map/ppermute | solution.py:26
  6.2 1.6 collective-permute-start.4
  7.8 4.8 %collective-permute-done = bf16[64,1024]{1,0:T(8,128)(2,1)S(1)} collective-permute-done((bf16[64,1024]{1,0:T(8,128)(2,1)S(1)}, bf16[64,1024]{1,0:T(8,128)(2,1)S(1)}, u32[]{:S(2)}, u32[]{:S(2)}) %collective-permute-start) | collective-permute-done | bytes 131104 | tf_op jit(solution)/shard_map/ppermute | solution.py:26
  12.6 0.7 collective-permute-start.1
  13.3 3.4 collective-permute-start.5
  16.9 8.3 %collective-permute-done.1 = bf16[2,64,1024]{2,1,0:T(8,128)(2,1)S(1)} collective-permute-done((bf16[2,64,1024]{2,1,0:T(8,128)(2,1)S(1)}, bf16[2,64,1024]{2,1,0:T(8,128)(2,1)S(1)}, u32[]{:S(2)}, u32[]{:S(2)}) %collective-permute-start.1) | collective-permute-done | bytes 262176 | tf_op jit(solution)/shard_map/ppermute | solution.py:26
  25.1 0.2 maximum_select_fusion.9
  25.3 1.5 collective-permute-start.2
  26.9 1.8 collective-permute-done.5
  28.7 1.6 collective-permute-start.6
  30.4 6.4 %collective-permute-done.2 = bf16[2,2,64,1024]{3,2,1,0:T(8,128)(2,1)S(1)} collective-permute-done((bf16[2,2,64,1024]{3,2,1,0:T(8,128)(2,1)S(1)}, bf16[2,2,64,1024]{3,2,1,0:T(8,128)(2,1)S(1)}, u32[]{:S(2)}, u32[]{:S(2)}) %collective-permute-start.2) | collective-permute-done | bytes 524320 | tf_op jit(solution)/shard_map/ppermute | solution.py:26
  37.0 1.3 collective-permute-start.3
  38.4 1.2 collective-permute-done.6
  39.6 0.2 maximum_select_fusion.6
  39.7 2.1 collective-permute-start.7
  42.0 0.2 maximum_select_fusion.3
  42.1 0.2 maximum_select_fusion.5
  42.3 18.1 %collective-permute-done.3 = bf16[2,2,2,64,1024]{4,3,1,0,2:T(8,128)(2,1)S(1)} collective-permute-done((bf16[2,2,2,64,1024]{4,3,1,0,2:T(8,128)(2,1)S(1)}, bf16[2,2,2,64,1024]{4,3,1,0,2:T(8,128)(2,1)S(1)}, u32[]{:S(2)}, u32[]{:S(2)}) %collective-permute-start.3) | collective-permute-done | bytes 1048608 | tf_op jit(solution)/shard_map/ppermute | solution.py:26
  60.5 0.3 maximum_select_fusion.1
  60.8 0.2 copy.28
  61.0 0.3 maximum_select_fusion.2
  61.4 0.2 copy.29
  61.6 3.6 fusion.15
  65.2 8.6 %collective-permute-start.10 = (bf16[4096,256]{1,0:T(8,128)(2,1)}, bf16[4096,256]{1,0:T(8,128)(2,1)}, u32[]{:S(2)}, u32[]{:S(2)}) collective-permute-start(bf16[4096,256]{1,0:T(8,128)(2,1)} %bitcast.34), channel_id=1, source_target_pairs={{1,0},{2,1},{3,2},{4,3},{5,4},{6,5},{7,6},{8,7},{9,8},{10,9},{11,1... | collective-permute-start | bytes 6291464 | tf_op jit(solution)/shard_map/ppermute | solution.py:20
  73.8 4.2 %reshape.691 = bf16[64,32,2,256]{3,2,1,0:T(2,128)(2,1)} reshape(bf16[1,64,64,256]{3,2,1,0:T(8,128)(2,1)} %param.7) | data formatting | bytes 4194304 | tf_op jit(solution)/shard_map/reshape | solution.py:175
  78.1 3.5 copy.32
  81.6 38.0 %collective-permute-done.10 = bf16[4096,256]{1,0:T(8,128)(2,1)} collective-permute-done((bf16[4096,256]{1,0:T(8,128)(2,1)}, bf16[4096,256]{1,0:T(8,128)(2,1)}, u32[]{:S(2)}, u32[]{:S(2)}) %collective-permute-start.10) | collective-permute-done | bytes 2097184 | tf_op jit(solution)/shard_map/ppermute | solution.py:20
  119.7 41.2 %collective-permute-done.9 = bf16[4096,256]{1,0:T(8,128)(2,1)} collective-permute-done((bf16[4096,256]{1,0:T(8,128)(2,1)}, bf16[4096,256]{1,0:T(8,128)(2,1)}, u32[]{:S(2)}, u32[]{:S(2)}) %collective-permute-start.9) | collective-permute-done | bytes 2097184 | tf_op jit(solution)/shard_map/ppermute | solution.py:19
  160.8 9.1 %pad_maximum_fusion.table_ref = bf16[12288,256]{1,0:T(8,128)(2,1)} fusion(bf16[4096,256]{1,0:T(8,128)(2,1)} %collective-permute-done.10, bf16[4096,256]{1,0:T(8,128)(2,1)} %bitcast.34, bf16[4096,256]{1,0:T(8,128)(2,1)} %collective-permute-done.9), kind=kLoop, calls=%fused_computation.3 | loop fusion | flops 18874368 | bytes 12582912 | tf_op jit(solution)/shard_map/concatenate | solution.py:21
  169.9 8.1 %maximum_select_fusion = bf16[16,2,2,64,1024]{4,3,0,2,1:T(8,128)(2,1)} fusion(bf16[16,1,2,64,1024]{4,3,0,2,1:T(8,128)(2,1)} %bitcast.30, bf16[16,1,2,64,1024]{4,3,0,2,1:T(8,128)(2,1)S(1)} %copy-done.4, pred[]{:T(512)S(6)} %eq.23), kind=kLoop, calls=%fused_computation | loop fusion | flops 12582912 | bytes 16777216 | tf_op jit(solution)/shard_map/jit(_where)/select_n | solution.py:36
  178.0 8.6 %copy.30 = bf16[16,2,2,64,1024]{4,3,2,1,0:T(8,128)(2,1)} copy(bf16[16,2,2,64,1024]{4,3,0,2,1:T(8,128)(2,1)} %maximum_select_fusion) | data formatting | bytes 16777216 | tf_op jit(solution)/shard_map/jit(_where)/select_n | solution.py:36
  186.6 14.5 %convert_bitcast_fusion.h_ref = bf16[1024,4096]{1,0:T(8,128)(2,1)} fusion(bf16[4096,1024]{1,0:T(8,128)(2,1)} %bitcast.121, bf16[1024,1024]{1,0:T(8,128)(2,1)S(1)} %bitcast.110), kind=kOutput, calls=%fused_computation.1 | convolution fusion | flops 8594128896 | bytes 18874368 | tf_op jit(solution)/shard_map/dot_general | solution.py:178
  201.2 36.4 %shard_map.77 = (bf16[1024,4096]{1,0:T(8,128)(2,1)}, f32[1,256]{1,0:T(1,128)S(1)}) custom-call(s32[1024]{0:T(1024)S(1)} %reshape.686.where_ref, s32[64]{0:T(128)S(1)} %bitcast.115, bf16[1024,4096]{1,0:T(8,128)(2,1)} %convert_bitcast_fusion.h_ref, bf16[12288,256]{1,0:T(8,128)(2,1)S(1)} %bitcast.113, bf16[4096,256]{1,0:T(8,128)(2,1)S(1)} %bitcast.114, ...), custom_call_target="tpu_custom_call" | custom-call | flops 8589934592 | bytes 16777216 | tf_op jit(solution)/shard_map/pallas_call | solution.py:138
  237.6 11.4 %convolution_convert_fusion = bf16[4096,1024]{1,0:T(8,128)(2,1)S(1)} fusion(bf16[1024,4096]{1,0:T(8,128)(2,1)} %get-tuple-element.5, bf16[1024,1024]{1,0:T(8,128)(2,1)S(1)} %bitcast.111), kind=kOutput, calls=%fused_computation.2 | convolution fusion | flops 8594128896 | bytes 18874368 | tf_op jit(solution)/shard_map/dot_general | solution.py:185
  249.0 1.5 fusion.16
  250.5 1.7 dynamic-slice_bitcast_fusion.1
  252.2 2.1 dynamic-slice_bitcast_fusion
  254.3 0.7 copy-done.7
  255.0 1.6 collective-permute-done.11
  256.7 3.2 convert_add_fusion.1
  260.0 2.5 collective-permute-start.12
  262.6 2.5 convert_add_fusion
  265.1 2.0 copy-done.8
  267.1 1.1 fusion.1
  268.2 17.9 %collective-permute-done.12 = bf16[2,2,2,64,1024]{4,3,2,1,0:T(8,128)(2,1)} collective-permute-done((bf16[2,2,2,64,1024]{4,3,2,1,0:T(8,128)(2,1)S(1)}, bf16[2,2,2,64,1024]{4,3,2,1,0:T(8,128)(2,1)}, u32[]{:S(2)}, u32[]{:S(2)}) %collective-permute-start.12) | collective-permute-done | bytes 1048608 | tf_op jit(solution)/shard_map/ppermute | solution.py:26
  286.1 2.2 bitcast_add_fusion.1
  288.5 6.0 %collective-permute-done.17 = bf16[2,2,2,64,1024]{4,3,2,1,0:T(8,128)(2,1)} collective-permute-done((bf16[2,2,2,64,1024]{4,3,2,1,0:T(8,128)(2,1)}, bf16[2,2,2,64,1024]{4,3,2,1,0:T(8,128)(2,1)}, u32[]{:S(2)}, u32[]{:S(2)}) %collective-permute-start.17) | collective-permute-done | bytes 1048608 | tf_op jit(solution)/shard_map/ppermute | solution.py:26
  294.6 1.7 bitcast_add_fusion
  296.3 1.3 copy-done.12
  297.6 1.8 collective-permute-start.18
  299.4 5.3 %collective-permute-done.13 = bf16[2,2,64,1024]{3,2,1,0:T(8,128)(2,1)} collective-permute-done((bf16[2,2,64,1024]{3,2,1,0:T(8,128)(2,1)S(1)}, bf16[2,2,64,1024]{3,2,1,0:T(8,128)(2,1)}, u32[]{:S(2)}, u32[]{:S(2)}) %collective-permute-start.13) | collective-permute-done | bytes 524320 | tf_op jit(solution)/shard_map/ppermute | solution.py:26
  304.7 1.5 bitcast_add_fusion.3
  306.2 2.2 collective-permute-start.14
  308.4 1.6 collective-permute-done.18
  310.0 1.5 bitcast_add_fusion.2
  311.6 2.2 collective-permute-start.19
  313.9 2.9 collective-permute-done.14
  316.8 0.9 collective-permute-start.15
  317.7 14.5 %collective-permute-done.19 = bf16[2,64,1024]{2,1,0:T(8,128)(2,1)S(1)} collective-permute-done((bf16[2,64,1024]{2,1,0:T(8,128)(2,1)S(1)}, bf16[2,64,1024]{2,1,0:T(8,128)(2,1)S(1)}, u32[]{:S(2)}, u32[]{:S(2)}) %collective-permute-start.19) | collective-permute-done | bytes 262176 | tf_op jit(solution)/shard_map/ppermute | solution.py:26
  332.4 2.9 collective-permute-done.15
  335.4 5.5 %collective-permute-done.20 = f32[64,1024]{1,0:T(8,128)S(1)} collective-permute-done((f32[64,1024]{1,0:T(8,128)S(1)}, f32[64,1024]{1,0:T(8,128)S(1)}, u32[]{:S(2)}, u32[]{:S(2)}) %collective-permute-start.20) | collective-permute-done | bytes 262176 | tf_op jit(solution)/shard_map/ppermute | solution.py:26
  341.1 42.5 %psum.7 = f32[1,256]{1,0:T(1,128)} all-reduce(f32[1,256]{1,0:T(1,128)S(1)} %get-tuple-element.4), channel_id=1, replica_groups=mesh['dp'=2,'space'=16] {'space'}, use_global_device_ids=true, to_apply=%region_0.1 | all-reduce | flops 256 | bytes 2048 | tf_op jit(solution)/shard_map/psum | solution.py:184
  383.6 2.3 maximum_select_fusion.7
  (72 shorter events, 2.1 us)
Async XLA Ops:
  0.6 186.0 %copy-start = (bf16[1,64,16,1024]{3,2,1,0:T(8,128)(2,1)S(1)}, bf16[1,64,16,1024]{3,2,1,0:T(8,128)(2,1)}, u32[]{:S(2)}) copy-start(bf16[1,64,16,1024]{3,2,1,0:T(8,128)(2,1)} %param.6) | copy-start | bytes 6291460
  2.1 10.5 %collective-permute-start = (bf16[64,1024]{1,0:T(8,128)(2,1)S(1)}, bf16[64,1024]{1,0:T(8,128)(2,1)S(1)}, u32[]{:S(2)}, u32[]{:S(2)}) collective-permute-start(bf16[64,1024]{1,0:T(8,128)(2,1)S(1)} %bitcast.128), channel_id=1, source_target_pairs={{0,8},{1,9},{2,10},{3,11},{4,12},{5,13},{6,14},{7,15},{8,0},{9,1},... | collective-permute-start | bytes 393224 | tf_op jit(solution)/shard_map/ppermute | solution.py:26
  6.2 7.1 %collective-permute-start.4 = (bf16[64,1024]{1,0:T(8,128)(2,1)S(1)}, bf16[64,1024]{1,0:T(8,128)(2,1)S(1)}, u32[]{:S(2)}, u32[]{:S(2)}) collective-permute-start(bf16[64,1024]{1,0:T(8,128)(2,1)S(1)} %bitcast.141), channel_id=1, source_target_pairs={{0,4},{1,5},{2,6},{3,7},{4,0},{5,1},{6,2},{7,3},{8,12},{9,13},{10,... | collective-permute-start | bytes 393224 | tf_op jit(solution)/shard_map/ppermute | solution.py:26
  12.6 12.5 %collective-permute-start.1 = (bf16[2,64,1024]{2,1,0:T(8,128)(2,1)S(1)}, bf16[2,64,1024]{2,1,0:T(8,128)(2,1)S(1)}, u32[]{:S(2)}, u32[]{:S(2)}) collective-permute-start(bf16[2,64,1024]{2,1,0:T(8,128)(2,1)S(1)} %maximum_select_fusion.13), channel_id=1, source_target_pairs={{0,4},{1,5},{2,6},{3,7},{4,0},{5,1},{6,2},{7,3},{8,12},{9,13},{10,... | collective-permute-start | bytes 786440 | tf_op jit(solution)/shard_map/ppermute | solution.py:26
  13.3 15.3 %collective-permute-start.5 = (bf16[2,64,1024]{2,1,0:T(8,128)(2,1)S(1)}, bf16[2,64,1024]{2,1,0:T(8,128)(2,1)S(1)}, u32[]{:S(2)}, u32[]{:S(2)}) collective-permute-start(bf16[2,64,1024]{2,1,0:T(8,128)(2,1)S(1)} %maximum_select_fusion.15), channel_id=1, source_target_pairs={{0,8},{1,9},{2,10},{3,11},{4,12},{5,13},{6,14},{7,15},{8,0},{9,1},... | collective-permute-start | bytes 786440 | tf_op jit(solution)/shard_map/ppermute | solution.py:26
  25.3 11.5 %collective-permute-start.2 = (bf16[2,2,64,1024]{3,2,1,0:T(8,128)(2,1)S(1)}, bf16[2,2,64,1024]{3,2,1,0:T(8,128)(2,1)S(1)}, u32[]{:S(2)}, u32[]{:S(2)}) collective-permute-start(bf16[2,2,64,1024]{3,2,1,0:T(8,128)(2,1)S(1)} %maximum_select_fusion.9), channel_id=1, source_target_pairs={{0,2},{1,3},{2,0},{3,1},{4,6},{5,7},{6,4},{7,5},{8,10},{9,11},{10,... | collective-permute-start | bytes 1572872 | tf_op jit(solution)/shard_map/ppermute | solution.py:26
  28.7 10.8 %collective-permute-start.6 = (bf16[2,2,64,1024]{3,2,1,0:T(8,128)(2,1)S(1)}, bf16[2,2,64,1024]{3,2,1,0:T(8,128)(2,1)S(1)}, u32[]{:S(2)}, u32[]{:S(2)}) collective-permute-start(bf16[2,2,64,1024]{3,2,1,0:T(8,128)(2,1)S(1)} %maximum_select_fusion.11), channel_id=1, source_target_pairs={{0,1},{1,0},{2,3},{3,2},{4,5},{5,4},{6,7},{7,6},{8,9},{9,8},{10,11... | collective-permute-start | bytes 1572872 | tf_op jit(solution)/shard_map/ppermute | solution.py:26
  37.0 23.5 %collective-permute-start.3 = (bf16[2,2,2,64,1024]{4,3,1,0,2:T(8,128)(2,1)S(1)}, bf16[2,2,2,64,1024]{4,3,1,0,2:T(8,128)(2,1)S(1)}, u32[]{:S(2)}, u32[]{:S(2)}) collective-permute-start(bf16[2,2,2,64,1024]{4,3,1,0,2:T(8,128)(2,1)S(1)} %maximum_select_fusion.4), channel_id=1, source_target_pairs={{0,1},{1,0},{2,3},{3,2},{4,5},{5,4},{6,7},{7,6},{8,9},{9,8},{10,11... | collective-permute-start | bytes 3145736 | tf_op jit(solution)/shard_map/ppermute | solution.py:26
  39.7 21.3 %collective-permute-start.7 = (bf16[2,2,2,64,1024]{4,3,1,0,2:T(8,128)(2,1)S(1)}, bf16[2,2,2,64,1024]{4,3,1,0,2:T(8,128)(2,1)S(1)}, u32[]{:S(2)}, u32[]{:S(2)}) collective-permute-start(bf16[2,2,2,64,1024]{4,3,1,0,2:T(8,128)(2,1)S(1)} %maximum_select_fusion.6), channel_id=1, source_target_pairs={{0,2},{1,3},{2,0},{3,1},{4,6},{5,7},{6,4},{7,5},{8,10},{9,11},{10,... | collective-permute-start | bytes 3145736 | tf_op jit(solution)/shard_map/ppermute | solution.py:26
  65.2 12.7 %copy-start.13 = (s32[1,64,16]{1,2,0:T(8,128)S(1)}, s32[1,64,16]{1,2,0:T(8,128)}, u32[]{:S(2)}) copy-start(s32[1,64,16]{1,2,0:T(8,128)} %param.8) | copy-start | bytes 12292
  65.2 104.7 %collective-permute-start.8 = (bf16[16,2,64,1024]{3,2,0,1:T(8,128)(2,1)}, bf16[16,2,64,1024]{3,2,0,1:T(8,128)(2,1)}, u32[]{:S(2)}, u32[]{:S(2)}) collective-permute-start(bf16[16,2,64,1024]{3,2,0,1:T(8,128)(2,1)} %get-tuple-element.9), channel_id=1, source_target_pairs={{0,16},{16,0},{1,17},{17,1},{2,18},{18,2},{3,19},{19,3},{4,20},{20... | collective-permute-start | bytes 12582920 | tf_op jit(solution)/shard_map/ppermute | solution.py:26
  65.2 54.4 %collective-permute-start.10 = (bf16[4096,256]{1,0:T(8,128)(2,1)}, bf16[4096,256]{1,0:T(8,128)(2,1)}, u32[]{:S(2)}, u32[]{:S(2)}) collective-permute-start(bf16[4096,256]{1,0:T(8,128)(2,1)} %bitcast.34), channel_id=1, source_target_pairs={{1,0},{2,1},{3,2},{4,3},{5,4},{6,5},{7,6},{8,7},{9,8},{10,9},{11,1... | collective-permute-start | bytes 6291464 | tf_op jit(solution)/shard_map/ppermute | solution.py:20
  73.8 87.0 %collective-permute-start.9 = (bf16[4096,256]{1,0:T(8,128)(2,1)}, bf16[4096,256]{1,0:T(8,128)(2,1)}, u32[]{:S(2)}, u32[]{:S(2)}) collective-permute-start(bf16[4096,256]{1,0:T(8,128)(2,1)} %bitcast.34), channel_id=1, source_target_pairs={{0,1},{1,2},{2,3},{3,4},{4,5},{5,6},{6,7},{7,8},{8,9},{9,10},{10,1... | collective-permute-start | bytes 6291464 | tf_op jit(solution)/shard_map/ppermute | solution.py:19
  81.6 88.3 %copy-start.4 = (bf16[16,1,2,64,1024]{4,3,0,2,1:T(8,128)(2,1)S(1)}, bf16[16,1,2,64,1024]{4,3,0,2,1:T(8,128)(2,1)}, u32[]{:S(2)}) copy-start(bf16[16,1,2,64,1024]{4,3,0,2,1:T(8,128)(2,1)} %get-tuple-element.8) | copy-start | bytes 12582916
  178.0 23.2 %slice-start = ((s8[6291456]{0:T(1024)(128)(4,1)}), s8[2097152]{0:T(1024)(128)(4,1)S(1)}, s32[]{:S(2)}) async-start(s8[6291456]{0:T(1024)(128)(4,1)} %bitcast.112), calls=%async_computation | async-start | bytes 4194304
  186.6 14.6 %slice-start.1 = ((s8[6291456]{0:T(1024)(128)(4,1)}), s8[4194304]{0:T(1024)(128)(4,1)S(1)}, s32[]{:S(2)}) async-start(s8[6291456]{0:T(1024)(128)(4,1)} %bitcast.112), calls=%async_computation.1 | async-start | bytes 8388608
  186.6 14.6 %copy-start.1 = (bf16[64,32,2,256]{3,1,2,0:T(8,128)(2,1)S(1)}, bf16[64,32,2,256]{3,1,2,0:T(8,128)(2,1)}, u32[]{:S(2)}) copy-start(bf16[64,32,2,256]{3,1,2,0:T(8,128)(2,1)} %copy.32) | copy-start | bytes 6291460
  186.6 14.6 %copy-start.2 = (f32[1,256]{1,0:T(1,128)S(1)}, f32[1,256]{1,0:T(1,128)}, u32[]{:S(2)}) copy-start(f32[1,256]{1,0:T(1,128)} %occ_ref.1) | copy-start | bytes 3076
  186.6 14.6 %copy-start.3 = (s32[1,64]{1,0:T(1,128)S(1)}, s32[1,64]{1,0:T(1,128)}, u32[]{:S(2)}) copy-start(s32[1,64]{1,0:T(1,128)} %param.9) | copy-start | bytes 772
  250.5 3.9 %copy-start.5 = (bf16[16,2,1,64,1024]{4,3,2,1,0:T(8,128)(2,1)}, bf16[16,2,1,64,1024]{4,3,2,1,0:T(8,128)(2,1)S(1)}, u32[]{:S(2)}) copy-start(bf16[16,2,1,64,1024]{4,3,2,1,0:T(8,128)(2,1)S(1)} %get-tuple-element.7) | copy-start | bytes 12582916
  250.5 4.5 %copy-start.7 = (bf16[16,2,1,64,1024]{4,3,2,1,0:T(8,128)(2,1)}, bf16[16,2,1,64,1024]{4,3,2,1,0:T(8,128)(2,1)S(1)}, u32[]{:S(2)}) copy-start(bf16[16,2,1,64,1024]{4,3,2,1,0:T(8,128)(2,1)S(1)} %get-tuple-element.6) | copy-start | bytes 12582916
  252.2 4.5 %collective-permute-start.11 = (bf16[16,64,1024]{2,1,0:T(8,128)(2,1)}, bf16[16,64,1024]{2,1,0:T(8,128)(2,1)}, u32[]{:S(2)}, u32[]{:S(2)}) collective-permute-start(bf16[16,64,1024]{2,1,0:T(8,128)(2,1)} %dynamic-slice_bitcast_fusion.1), channel_id=1, source_target_pairs={{0,16},{16,0},{1,17},{17,1},{2,18},{18,2},{3,19},{19,3},{4,20},{20... | collective-permute-start | bytes 6291464 | tf_op jit(solution)/shard_map/ppermute | solution.py:26
  255.0 7.6 %collective-permute-start.16 = (bf16[16,64,1024]{2,1,0:T(8,128)(2,1)}, bf16[16,64,1024]{2,1,0:T(8,128)(2,1)}, u32[]{:S(2)}, u32[]{:S(2)}) collective-permute-start(bf16[16,64,1024]{2,1,0:T(8,128)(2,1)} %dynamic-slice_bitcast_fusion), channel_id=1, source_target_pairs={{0,16},{16,0},{1,17},{17,1},{2,18},{18,2},{3,19},{19,3},{4,20},{20... | collective-permute-start | bytes 6291464 | tf_op jit(solution)/shard_map/ppermute | solution.py:26
  255.0 7.6 %copy-start.6 = (bf16[16,2,1,64,1024]{4,3,2,1,0:T(8,128)(2,1)S(1)}, bf16[16,2,1,64,1024]{4,3,2,1,0:T(8,128)(2,1)}, u32[]{:S(2)}) copy-start(bf16[16,2,1,64,1024]{4,3,2,1,0:T(8,128)(2,1)} %copy-done.5) | copy-start | bytes 12582916
  259.8 2.7 copy-start.10
  260.0 26.1 %collective-permute-start.12 = (bf16[2,2,2,64,1024]{4,3,2,1,0:T(8,128)(2,1)S(1)}, bf16[2,2,2,64,1024]{4,3,2,1,0:T(8,128)(2,1)}, u32[]{:S(2)}, u32[]{:S(2)}) collective-permute-start(bf16[2,2,2,64,1024]{4,3,2,1,0:T(8,128)(2,1)S(1)} %fusion), channel_id=1, source_target_pairs={{0,1},{1,0},{2,3},{3,2},{4,5},{5,4},{6,7},{7,6},{8,9},{9,8},{10,11... | collective-permute-start | bytes 3145736 | tf_op jit(solution)/shard_map/ppermute | solution.py:26
  265.1 2.0 copy-start.8
  268.2 26.4 %collective-permute-start.17 = (bf16[2,2,2,64,1024]{4,3,2,1,0:T(8,128)(2,1)}, bf16[2,2,2,64,1024]{4,3,2,1,0:T(8,128)(2,1)}, u32[]{:S(2)}, u32[]{:S(2)}) collective-permute-start(bf16[2,2,2,64,1024]{4,3,2,1,0:T(8,128)(2,1)} %fusion.1), channel_id=1, source_target_pairs={{0,2},{1,3},{2,0},{3,1},{4,6},{5,7},{6,4},{7,5},{8,10},{9,11},{10,... | collective-permute-start | bytes 3145736 | tf_op jit(solution)/shard_map/ppermute | solution.py:26
  268.2 26.4 %copy-start.9 = (f32[16,64,1024]{2,1,0:T(8,128)S(1)}, f32[16,64,1024]{2,1,0:T(8,128)}, u32[]{:S(2)}) copy-start(f32[16,64,1024]{2,1,0:T(8,128)} %copy-done.8) | copy-start | bytes 12582916
  288.4 7.9 %copy-start.11 = (f32[2,2,2,64,1024]{4,3,2,1,0:T(8,128)}, f32[2,2,2,64,1024]{4,3,2,1,0:T(8,128)S(1)}, u32[]{:S(2)}) copy-start(f32[2,2,2,64,1024]{4,3,2,1,0:T(8,128)S(1)} %bitcast_add_fusion.1) | copy-start | bytes 6291460
  288.5 16.2 %collective-permute-start.13 = (bf16[2,2,64,1024]{3,2,1,0:T(8,128)(2,1)S(1)}, bf16[2,2,64,1024]{3,2,1,0:T(8,128)(2,1)}, u32[]{:S(2)}, u32[]{:S(2)}) collective-permute-start(bf16[2,2,64,1024]{3,2,1,0:T(8,128)(2,1)S(1)} %fusion.2), channel_id=1, source_target_pairs={{0,2},{1,3},{2,0},{3,1},{4,6},{5,7},{6,4},{7,5},{8,10},{9,11},{10,... | collective-permute-start | bytes 1572872 | tf_op jit(solution)/shard_map/ppermute | solution.py:26
  296.3 1.4 copy-start.12
  297.6 12.4 %collective-permute-start.18 = (bf16[2,2,64,1024]{3,2,1,0:T(8,128)(2,1)S(1)}, bf16[2,2,64,1024]{3,2,1,0:T(8,128)(2,1)}, u32[]{:S(2)}, u32[]{:S(2)}) collective-permute-start(bf16[2,2,64,1024]{3,2,1,0:T(8,128)(2,1)S(1)} %fusion.3), channel_id=1, source_target_pairs={{0,1},{1,0},{2,3},{3,2},{4,5},{5,4},{6,7},{7,6},{8,9},{9,8},{10,11... | collective-permute-start | bytes 1572872 | tf_op jit(solution)/shard_map/ppermute | solution.py:26
  306.2 10.5 %collective-permute-start.14 = (bf16[2,64,1024]{2,1,0:T(8,128)(2,1)S(1)}, bf16[2,64,1024]{2,1,0:T(8,128)(2,1)S(1)}, u32[]{:S(2)}, u32[]{:S(2)}) collective-permute-start(bf16[2,64,1024]{2,1,0:T(8,128)(2,1)S(1)} %fusion.4), channel_id=1, source_target_pairs={{0,4},{1,5},{2,6},{3,7},{4,0},{5,1},{6,2},{7,3},{8,12},{9,13},{10,... | collective-permute-start | bytes 786440 | tf_op jit(solution)/shard_map/ppermute | solution.py:26
  311.6 20.6 %collective-permute-start.19 = (bf16[2,64,1024]{2,1,0:T(8,128)(2,1)S(1)}, bf16[2,64,1024]{2,1,0:T(8,128)(2,1)S(1)}, u32[]{:S(2)}, u32[]{:S(2)}) collective-permute-start(bf16[2,64,1024]{2,1,0:T(8,128)(2,1)S(1)} %fusion.5), channel_id=1, source_target_pairs={{0,8},{1,9},{2,10},{3,11},{4,12},{5,13},{6,14},{7,15},{8,0},{9,1},... | collective-permute-start | bytes 786440 | tf_op jit(solution)/shard_map/ppermute | solution.py:26
  316.8 18.5 %collective-permute-start.15 = (f32[64,1024]{1,0:T(8,128)S(1)}, f32[64,1024]{1,0:T(8,128)S(1)}, u32[]{:S(2)}, u32[]{:S(2)}) collective-permute-start(f32[64,1024]{1,0:T(8,128)S(1)} %dynamic-slice_bitcast_fusion.3), channel_id=1, source_target_pairs={{0,8},{1,9},{2,10},{3,11},{4,12},{5,13},{6,14},{7,15},{8,0},{9,1},... | collective-permute-start | bytes 786440 | tf_op jit(solution)/shard_map/ppermute | solution.py:26
  332.3 8.5 %collective-permute-start.20 = (f32[64,1024]{1,0:T(8,128)S(1)}, f32[64,1024]{1,0:T(8,128)S(1)}, u32[]{:S(2)}, u32[]{:S(2)}) collective-permute-start(f32[64,1024]{1,0:T(8,128)S(1)} %dynamic-slice_bitcast_fusion.2), channel_id=1, source_target_pairs={{0,4},{1,5},{2,6},{3,7},{4,0},{5,1},{6,2},{7,3},{8,12},{9,13},{10,... | collective-permute-start | bytes 786440 | tf_op jit(solution)/shard_map/ppermute | solution.py:26
  341.0 42.6 %collective-permute-start.21 = (f32[2,64,1024]{2,1,0:T(8,128)S(1)}, f32[2,64,1024]{2,1,0:T(8,128)}, u32[]{:S(2)}, u32[]{:S(2)}) collective-permute-start(f32[2,64,1024]{2,1,0:T(8,128)S(1)} %get-tuple-element.11), channel_id=1, source_target_pairs={{0,16},{16,0},{1,17},{17,1},{2,18},{18,2},{3,19},{19,3},{4,20},{20... | collective-permute-start | bytes 1572872 | tf_op jit(solution)/shard_map/ppermute | solution.py:26

commit v3 on v2

--- a/solution.py
+++ b/solution.py
@@ -10,15 +10,16 @@
 
 GROUP = 4
 PITCH = 40
-
-
-def with_halo(value, axis, dim):
+PIECES = 4
+
+
+def halo_pieces(value, axis):
     size = lax.axis_size(axis)
-    up = [(i, (i + 1) % size) for i in range(size)]
-    down = [(j, i) for i, j in up]
-    before = lax.ppermute(value, axis, up)
-    after = lax.ppermute(value, axis, down)
-    return jnp.concatenate([before, value, after], axis=dim)
+    across = [(i, i ^ 1) for i in range(size)]
+    along = [(i, (i + 2 - 4 * (i % 2)) % size) for i in range(size)]
+    near = [lax.ppermute(piece, axis, across) for piece in jnp.split(value, PIECES)]
+    far = [lax.ppermute(piece, axis, along) for piece in near]
+    return near + [value] + far
 
 
 def swap(value, axis, bit):
@@ -76,8 +77,9 @@
 
 
 def tile_kernel(
-    group, slots, orbit, factor, where_ref, count_ref, h_ref, table_ref, own_ref, occ_ref, d_ref, energy_ref, spread, back, acc
+    group, slots, orbit, factor, where_ref, count_ref, h_ref, own_ref, occ_ref, *rest
 ):
+    *pieces, d_ref, energy_ref, spread, back, acc, table_ref, sems = rest
     step = pl.program_id(0)
     half = orbit // 2
     lanes = 2 * orbit
@@ -85,6 +87,15 @@
     @pl.when(step == 0)
     def _():
         acc[...] = jnp.zeros_like(acc)
+        copies, at = [], 0
+        for n, piece in enumerate(pieces):
+            size = piece.shape[0]
+            copies.append(pltpu.make_async_copy(piece, table_ref.at[pl.ds(at, size), :], sems.at[n]))
+            at += size
+        for copy in copies:
+            copy.start()
+        for copy in copies:
+            copy.wait()
 
     low = lax.broadcasted_iota(jnp.int32, (half, 2 * lanes), 1) % lanes < orbit
     slot = lax.broadcasted_iota(jnp.int32, (slots, 1), 0)
@@ -129,9 +140,9 @@
         energy_ref[...] = factor * jnp.sum(acc[...], axis=0, keepdims=True)
 
 
-def tiles(blocks, table, own, occupation, where, counts, slots, orbit, factor):
+def tiles(blocks, pieces, own, occupation, where, counts, slots, orbit, factor):
     count = counts.shape[0]
-    bands = table.shape[1]
+    bands = own.shape[1]
     group = GROUP
     rows, square = blocks.shape
     flops = 2 * rows * square * bands * 4
@@ -146,9 +157,9 @@
             grid=(count // group,),
             in_specs=[
                 pl.BlockSpec((group * slots, square), lambda i, *_: (i, 0)),
-                pl.BlockSpec(table.shape, lambda i, *_: (0, 0), pipeline_mode=pl.Buffered(1)),
                 pl.BlockSpec((group * orbit, bands), lambda i, *_: (i, 0)),
                 pl.BlockSpec((1, bands), lambda i, *_: (0, 0)),
+                *[pl.BlockSpec(memory_space=pl.ANY) for _ in pieces],
             ],
             out_specs=[
                 pl.BlockSpec((group * slots, square), lambda i, *_: (i, 0)),
@@ -158,11 +169,13 @@
                 pltpu.VMEM((group, slots * PITCH, 2 * orbit), jnp.float32),
                 pltpu.VMEM((group, slots * PITCH, 2 * orbit), jnp.float32),
                 pltpu.VMEM((orbit, bands), jnp.float32),
+                pltpu.VMEM((sum(piece.shape[0] for piece in pieces), bands), jnp.bfloat16),
+                pltpu.SemaphoreType.DMA((len(pieces),)),
             ],
         ),
         compiler_params=pltpu.CompilerParams(vmem_limit_bytes=40 * 2**20),
         cost_estimate=pl.CostEstimate(flops=flops, bytes_accessed=4 * rows * square, transcendentals=0),
-    )(where, counts, blocks, table, own, occupation)
+    )(where, counts, blocks, own, occupation, *pieces)
 
 
 def local(features, psi, neighbors, counts, occupation, weights):
@@ -173,15 +186,19 @@
     factor = 1.0 / math.sqrt(rows * nspace * slots)
     flat = features.reshape(rows * slots, width)
     own = psi.reshape(rows, orbit // 2, 2, bands).swapaxes(1, 2).reshape(rows * orbit, bands)
-    table = with_halo(psi.reshape(rows * orbit, bands), "space", 0)
-    where = (neighbors // rows - myself + 1 + nspace) % nspace * rows + neighbors % rows
+    pieces = halo_pieces(psi.reshape(rows * orbit, bands), "space")
+    offset = (neighbors // rows - myself + 1 + nspace) % nspace
+    offset = jnp.where(myself % 2 == 0, 2 - offset, offset)
+    where = offset * rows + neighbors % rows
     blocks = lax.dot_general(
         flat, gather_rows(weights.T), (((1,), (1,)), ((), ())), preferred_element_type=jnp.float32
     ).astype(jnp.bfloat16)
     dblocks, energy = tiles(
-        blocks, table, own, occupation, where.reshape(-1), counts.reshape(-1), slots, orbit, factor
+        blocks, pieces, own, occupation, where.reshape(-1), counts.reshape(-1), slots, orbit, factor
     )
-    energies = lax.psum(energy, "space")
+    energies = energy
+    for bit in chains(nspace)[0]:
+        energies = energies + swap(energies, "space", bit)
     partial = lax.dot_general(dblocks, flat, (((0,), (0,)), ((), ())), preferred_element_type=jnp.float32)
     gradient = scatter_rows(partial.astype(jnp.bfloat16))
     return (energies, gradient)

time: 386 us -> 313 us (0.81)
  blocking collectives: 42.5 us -> 0 us
  waiting for transfers between devices: 178 us -> 147 us
  other arithmetic: 38.1 us -> 30.1 us
  starting transfers between devices: 34.8 us -> 41.1 us
    ppermute x2 -> x8, waiting for transfers between devices: 79.2 us -> 32 us  [the longest x4 32 us: halo_pieces(): lax.ppermute(piece, axis, across)]
    psum x1 -> x0, blocking collectives: 42.5 us -> none  [local(): energies = lax.psum(energy, 'space')]
    ppermute x20 -> x24, waiting for transfers between devices: 98.9 us -> 115 us  [swap(): return lax.ppermute(value, axis, [(i, i ^ 1 << bit) for i in range(size)])]
    concatenate x1 -> x0, other arithmetic: 9.1 us -> none  [with_halo(): return jnp.concatenate([before, value, after], axis=dim)]
    ppermute x20 -> x24, starting transfers between devices: 26.2 us -> 30.9 us  [swap(): return lax.ppermute(value, axis, [(i, i ^ 1 << bit) for i in range(size)])]
    ppermute x2 -> x8, starting transfers between devices: 8.57 us -> 10.1 us  [the longest x4 6.09 us: halo_pieces(): far = [lax.ppermute(piece, axis, along) for piece in near]]
  transfers between devices with their start and end apart: 22 -> 32, of which waited for: 17 -> 23; matrix products, arithmetic and copies ran while one was open for 9% -> 19% of each run, Pallas kernels for 0% -> 0%
where the time goes in v3:
time: 313 us; the launch traced here: 312 us
  waiting for transfers between devices  147 us (47%)
  starting transfers between devices  41.1 us (13%)
  Pallas kernels  37.5 us (12%)
  other arithmetic  30.1 us (10%)
  local copies, waits for them, and re-layouts  29.9 us (10%)
  matrix products  25.9 us (8%)
    ppermute x24, waiting for transfers between devices, swap(): return lax.ppermute(value, axis, [(i, i ^ 1 << bit) for i in range(size)])  115 us
    pallas_call x1, Pallas kernels, tiles(): pl.pallas_call(functools.partial(tile_kernel, group, slots, orbit, factor...  37.5 us
    ppermute x4, waiting for transfers between devices, halo_pieces(): lax.ppermute(piece, axis, across)  32 us
    ppermute x24, starting transfers between devices, swap(): return lax.ppermute(value, axis, [(i, i ^ 1 << bit) for i in range(size)])  30.9 us
    dot_general x1, matrix products, local(): lax.dot_general(flat, gather_rows(weights.T), (((1,), (1,)), ((), ())), p...  14.5 us
    select_n x17, other arithmetic, pair(): jnp.where(mybit == 0, jnp.stack([mine, theirs], axis), jnp.stack([theirs,...  13.4 us
    dot_general x1, matrix products, local(): lax.dot_general(dblocks, flat, (((0,), (0,)), ((), ())), preferred_elemen...  11.4 us
    select_n x3, local copies, waits for them, and re-layouts, pair(): jnp.where(mybit == 0, jnp.stack([mine, theirs], axis), jnp.stack([theirs,...  8.91 us
  transfers between devices with their start and end apart: 32, of which 23 were waited for; matrix products, arithmetic and copies ran while one was open for 19% of the time, Pallas kernels for 0%

profile of v3, /device:TPU:0, one launch (start us, length us, event | category | flops | bytes accessed | tf_op | source)
XLA Modules:
  0.0 312.4 jit_solution(16449355394509819658)
XLA Ops:
  0.7 1.4 copy.24
  2.1 4.1 %collective-permute-start = (bf16[64,1024]{1,0:T(8,128)(2,1)S(1)}, bf16[64,1024]{1,0:T(8,128)(2,1)S(1)}, u32[]{:S(2)}, u32[]{:S(2)}) collective-permute-start(bf16[64,1024]{1,0:T(8,128)(2,1)S(1)} %bitcast.131), channel_id=1, source_target_pairs={{0,8},{1,9},{2,10},{3,11},{4,12},{5,13},{6,14},{7,15},{8,0},{9,1},... | collective-permute-start | bytes 393224 | tf_op jit(solution)/shard_map/ppermute | solution.py:27
  6.2 1.6 collective-permute-start.4
  7.8 4.8 %collective-permute-done = bf16[64,1024]{1,0:T(8,128)(2,1)S(1)} collective-permute-done((bf16[64,1024]{1,0:T(8,128)(2,1)S(1)}, bf16[64,1024]{1,0:T(8,128)(2,1)S(1)}, u32[]{:S(2)}, u32[]{:S(2)}) %collective-permute-start) | collective-permute-done | bytes 131104 | tf_op jit(solution)/shard_map/ppermute | solution.py:27
  13.3 3.4 %collective-permute-start.5 = (bf16[2,64,1024]{2,1,0:T(8,128)(2,1)S(1)}, bf16[2,64,1024]{2,1,0:T(8,128)(2,1)S(1)}, u32[]{:S(2)}, u32[]{:S(2)}) collective-permute-start(bf16[2,64,1024]{2,1,0:T(8,128)(2,1)S(1)} %maximum_select_fusion.15), channel_id=1, source_target_pairs={{0,8},{1,9},{2,10},{3,11},{4,12},{5,13},{6,14},{7,15},{8,0},{9,1},... | collective-permute-start | bytes 786440 | tf_op jit(solution)/shard_map/ppermute | solution.py:27
  16.9 8.3 %collective-permute-done.1 = bf16[2,64,1024]{2,1,0:T(8,128)(2,1)S(1)} collective-permute-done((bf16[2,64,1024]{2,1,0:T(8,128)(2,1)S(1)}, bf16[2,64,1024]{2,1,0:T(8,128)(2,1)S(1)}, u32[]{:S(2)}, u32[]{:S(2)}) %collective-permute-start.1) | collective-permute-done | bytes 262176 | tf_op jit(solution)/shard_map/ppermute | solution.py:27
  25.3 1.5 collective-permute-start.2
  26.9 1.8 collective-permute-done.5
  28.7 1.6 collective-permute-start.6
  30.4 6.4 %collective-permute-done.2 = bf16[2,2,64,1024]{3,2,1,0:T(8,128)(2,1)S(1)} collective-permute-done((bf16[2,2,64,1024]{3,2,1,0:T(8,128)(2,1)S(1)}, bf16[2,2,64,1024]{3,2,1,0:T(8,128)(2,1)S(1)}, u32[]{:S(2)}, u32[]{:S(2)}) %collective-permute-start.2) | collective-permute-done | bytes 524320 | tf_op jit(solution)/shard_map/ppermute | solution.py:27
  37.0 1.3 collective-permute-start.3
  38.4 1.2 collective-permute-done.6
  39.7 2.1 collective-permute-start.7
  42.3 18.1 %collective-permute-done.3 = bf16[2,2,2,64,1024]{4,3,1,0,2:T(8,128)(2,1)S(1)} collective-permute-done((bf16[2,2,2,64,1024]{4,3,1,0,2:T(8,128)(2,1)S(1)}, bf16[2,2,2,64,1024]{4,3,1,0,2:T(8,128)(2,1)S(1)}, u32[]{:S(2)}, u32[]{:S(2)}) %collective-permute-start.3) | collective-permute-done | bytes 1048608 | tf_op jit(solution)/shard_map/ppermute | solution.py:27
  61.6 3.5 %fusion.15 = (bf16[16,1,2,64,1024]{4,3,0,2,1:T(8,128)(2,1)}, bf16[16,2,64,1024]{3,2,0,1:T(8,128)(2,1)}) fusion(bf16[16,1,64,1024]{3,2,0,1:T(8,128)(2,1)S(1)} %bitcast.126, bf16[16,1,64,1024]{3,2,0,1:T(8,128)(2,1)S(1)} %bitcast.125), kind=kLoop, calls=%fused_computation.68 | loop fusion | flops 2097152 | bytes 12582912 | tf_op jit(solution)/shard_map/stack | solution.py:37
  65.2 1.4 fusion.17
  66.6 1.5 collective-permute-start.9
  68.6 1.5 collective-permute-start.11
  70.7 4.1 %reshape.694 = bf16[64,32,2,256]{3,2,1,0:T(2,128)(2,1)} reshape(bf16[1,64,64,256]{3,2,1,0:T(8,128)(2,1)} %param.7) | data formatting | bytes 4194304 | tf_op jit(solution)/shard_map/reshape | solution.py:188
  74.9 3.4 %copy.32 = bf16[64,32,2,256]{3,1,2,0:T(8,128)(2,1)} copy(bf16[64,32,2,256]{3,2,1,0:T(2,128)(2,1)} %reshape.694) | data formatting | bytes 4194304 | tf_op jit(solution)/shard_map/reshape | solution.py:188
  78.4 3.2 %collective-permute-done.9.rest_0_ = bf16[1024,256]{1,0:T(8,128)(2,1)S(1)} collective-permute-done((bf16[1024,256]{1,0:T(8,128)(2,1)}, bf16[1024,256]{1,0:T(8,128)(2,1)S(1)}, u32[]{:S(2)}, u32[]{:S(2)}) %collective-permute-start.9) | collective-permute-done | bytes 524320 | tf_op jit(solution)/shard_map/ppermute | solution.py:20
  81.5 1.5 collective-permute-start.13
  83.1 9.7 %collective-permute-done.10.rest_1_ = bf16[1024,256]{1,0:T(8,128)(2,1)S(1)} collective-permute-done((bf16[1024,256]{1,0:T(8,128)(2,1)}, bf16[1024,256]{1,0:T(8,128)(2,1)S(1)}, u32[]{:S(2)}, u32[]{:S(2)}) %collective-permute-start.10) | collective-permute-done | bytes 524320 | tf_op jit(solution)/shard_map/ppermute | solution.py:20
  92.8 1.5 collective-permute-start.14
  94.3 9.8 %collective-permute-done.11.rest_2_ = bf16[1024,256]{1,0:T(8,128)(2,1)} collective-permute-done((bf16[1024,256]{1,0:T(8,128)(2,1)}, bf16[1024,256]{1,0:T(8,128)(2,1)}, u32[]{:S(2)}, u32[]{:S(2)}) %collective-permute-start.11) | collective-permute-done | bytes 524320 | tf_op jit(solution)/shard_map/ppermute | solution.py:20
  104.1 1.5 collective-permute-start.15
  105.6 9.3 %collective-permute-done.12.rest_3_ = bf16[1024,256]{1,0:T(8,128)(2,1)} collective-permute-done((bf16[1024,256]{1,0:T(8,128)(2,1)}, bf16[1024,256]{1,0:T(8,128)(2,1)}, u32[]{:S(2)}, u32[]{:S(2)}) %collective-permute-start.12) | collective-permute-done | bytes 524320 | tf_op jit(solution)/shard_map/ppermute | solution.py:20
  115.0 1.5 collective-permute-start.16
  116.5 10.4 %maximum_select_fusion = bf16[16,2,2,64,1024]{4,3,0,2,1:T(8,128)(2,1)} fusion(bf16[16,1,2,64,1024]{4,3,0,2,1:T(8,128)(2,1)} %bitcast.30, bf16[16,1,2,64,1024]{4,3,0,2,1:T(8,128)(2,1)} %get-tuple-element.8, pred[]{:T(512)S(6)} %eq.29), kind=kLoop, calls=%fused_computation | loop fusion | flops 12582912 | bytes 16777216 | tf_op jit(solution)/shard_map/jit(_where)/select_n | solution.py:37
  126.9 8.5 %copy.30 = bf16[16,2,2,64,1024]{4,3,2,1,0:T(8,128)(2,1)} copy(bf16[16,2,2,64,1024]{4,3,0,2,1:T(8,128)(2,1)} %maximum_select_fusion) | data formatting | bytes 16777216 | tf_op jit(solution)/shard_map/jit(_where)/select_n | solution.py:37
  135.4 14.5 %convert_bitcast_fusion.h_ref = bf16[1024,4096]{1,0:T(8,128)(2,1)} fusion(bf16[4096,1024]{1,0:T(8,128)(2,1)} %bitcast.124, bf16[1024,1024]{1,0:T(8,128)(2,1)S(1)} %bitcast.114), kind=kOutput, calls=%fused_computation.1 | convolution fusion | flops 8594128896 | bytes 18874368 | tf_op jit(solution)/shard_map/dot_general | solution.py:193
  149.9 37.5 %shard_map.77 = (bf16[1024,4096]{1,0:T(8,128)(2,1)}, f32[1,256]{1,0:T(1,128)S(1)}) custom-call(s32[1024]{0:T(1024)S(1)} %reshape.690.where_ref, s32[64]{0:T(128)S(1)} %bitcast.118, bf16[1024,4096]{1,0:T(8,128)(2,1)} %convert_bitcast_fusion.h_ref, bf16[4096,256]{1,0:T(8,128)(2,1)S(1)} %bitcast.117, f32[1,256]{1,0:T(1,128)S(1)} %copy-done.5, ...), custom_call_target="tpu_custom_call" | custom-call | flops 8589934592 | bytes 16777216 | tf_op jit(solution)/shard_map/pallas_call | solution.py:149
  187.5 11.4 %convolution_convert_fusion = bf16[4096,1024]{1,0:T(8,128)(2,1)S(1)} fusion(bf16[1024,4096]{1,0:T(8,128)(2,1)} %get-tuple-element.5, bf16[1024,1024]{1,0:T(8,128)(2,1)S(1)} %bitcast.115), kind=kOutput, calls=%fused_computation.2 | convolution fusion | flops 8594128896 | bytes 18874368 | tf_op jit(solution)/shard_map/dot_general | solution.py:202
  198.9 1.7 fusion.16
  200.6 1.7 dynamic-slice_bitcast_fusion.1
  203.4 1.1 copy-done.9
  204.5 2.3 collective-permute-done.21
  206.8 3.3 %convert_add_fusion.1 = f32[16,64,1024]{2,1,0:T(8,128)S(1)} fusion(bf16[16,64,1024]{2,1,0:T(8,128)(2,1)} %collective-permute-done.21, bf16[16,2,1,64,1024]{4,3,2,1,0:T(8,128)(2,1)} %copy-done.9, s32[]{:T(128)S(6)} %select_n.298), kind=kLoop, calls=%fused_computation.5 | loop fusion | flops 3145728 | bytes 8388612 | tf_op jit(solution)/shard_map/add | solution.py:64
  210.3 7.7 %collective-permute-start.22 = (bf16[2,2,2,64,1024]{4,3,2,1,0:T(8,128)(2,1)S(1)}, bf16[2,2,2,64,1024]{4,3,2,1,0:T(8,128)(2,1)}, u32[]{:S(2)}, u32[]{:S(2)}) collective-permute-start(bf16[2,2,2,64,1024]{4,3,2,1,0:T(8,128)(2,1)S(1)} %fusion), channel_id=1, source_target_pairs={{0,1},{1,0},{2,3},{3,2},{4,5},{5,4},{6,7},{7,6},{8,9},{9,8},{10,11... | collective-permute-start | bytes 3145736 | tf_op jit(solution)/shard_map/ppermute | solution.py:27
  218.0 2.5 convert_add_fusion
  220.5 2.0 copy-done.10
  222.5 1.1 fusion.1
  223.6 17.9 %collective-permute-done.22 = bf16[2,2,2,64,1024]{4,3,2,1,0:T(8,128)(2,1)} collective-permute-done((bf16[2,2,2,64,1024]{4,3,2,1,0:T(8,128)(2,1)S(1)}, bf16[2,2,2,64,1024]{4,3,2,1,0:T(8,128)(2,1)}, u32[]{:S(2)}, u32[]{:S(2)}) %collective-permute-start.22) | collective-permute-done | bytes 1048608 | tf_op jit(solution)/shard_map/ppermute | solution.py:27
  241.6 2.4 bitcast_add_fusion.1
  244.1 5.9 %collective-permute-done.27 = bf16[2,2,2,64,1024]{4,3,2,1,0:T(8,128)(2,1)} collective-permute-done((bf16[2,2,2,64,1024]{4,3,2,1,0:T(8,128)(2,1)}, bf16[2,2,2,64,1024]{4,3,2,1,0:T(8,128)(2,1)}, u32[]{:S(2)}, u32[]{:S(2)}) %collective-permute-start.27) | collective-permute-done | bytes 1048608 | tf_op jit(solution)/shard_map/ppermute | solution.py:27
  250.0 1.7 bitcast_add_fusion
  251.7 1.3 copy-done.13
  253.1 1.8 collective-permute-start.28
  254.9 5.2 %collective-permute-done.23 = bf16[2,2,64,1024]{3,2,1,0:T(8,128)(2,1)} collective-permute-done((bf16[2,2,64,1024]{3,2,1,0:T(8,128)(2,1)S(1)}, bf16[2,2,64,1024]{3,2,1,0:T(8,128)(2,1)}, u32[]{:S(2)}, u32[]{:S(2)}) %collective-permute-start.23) | collective-permute-done | bytes 524320 | tf_op jit(solution)/shard_map/ppermute | solution.py:27
  260.1 1.2 bitcast_add_fusion.3
  261.4 4.2 %collective-permute-done.28 = bf16[2,2,64,1024]{3,2,1,0:T(8,128)(2,1)} collective-permute-done((bf16[2,2,64,1024]{3,2,1,0:T(8,128)(2,1)S(1)}, bf16[2,2,64,1024]{3,2,1,0:T(8,128)(2,1)}, u32[]{:S(2)}, u32[]{:S(2)}) %collective-permute-start.28) | collective-permute-done | bytes 524320 | tf_op jit(solution)/shard_map/ppermute | solution.py:27
  265.6 1.2 bitcast_add_fusion.2
  266.9 2.4 collective-permute-done.24
  269.4 1.3 collective-permute-start.25
  270.7 14.6 %collective-permute-done.29 = bf16[2,64,1024]{2,1,0:T(8,128)(2,1)S(1)} collective-permute-done((bf16[2,64,1024]{2,1,0:T(8,128)(2,1)S(1)}, bf16[2,64,1024]{2,1,0:T(8,128)(2,1)S(1)}, u32[]{:S(2)}, u32[]{:S(2)}) %collective-permute-start.29) | collective-permute-done | bytes 262176 | tf_op jit(solution)/shard_map/ppermute | solution.py:27
  285.5 4.4 %collective-permute-done.25 = f32[64,1024]{1,0:T(8,128)S(1)} collective-permute-done((f32[64,1024]{1,0:T(8,128)S(1)}, f32[64,1024]{1,0:T(8,128)S(1)}, u32[]{:S(2)}, u32[]{:S(2)}) %collective-permute-start.25) | collective-permute-done | bytes 262176 | tf_op jit(solution)/shard_map/ppermute | solution.py:27
  289.9 5.5 %collective-permute-done.30 = f32[64,1024]{1,0:T(8,128)S(1)} collective-permute-done((f32[64,1024]{1,0:T(8,128)S(1)}, f32[64,1024]{1,0:T(8,128)S(1)}, u32[]{:S(2)}, u32[]{:S(2)}) %collective-permute-start.30) | collective-permute-done | bytes 262176 | tf_op jit(solution)/shard_map/ppermute | solution.py:27
  295.5 2.0 collective-permute-start.17
  297.6 1.6 collective-permute-done.17
  299.2 1.4 collective-permute-start.18
  300.6 2.1 collective-permute-done.18
  302.8 3.6 %collective-permute-done.19 = f32[1,256]{1,0:T(1,128)S(1)} collective-permute-done((f32[1,256]{1,0:T(1,128)S(1)}, f32[1,256]{1,0:T(1,128)S(1)}, u32[]{:S(2)}, u32[]{:S(2)}) %collective-permute-start.19) | collective-permute-done | bytes 1056 | tf_op jit(solution)/shard_map/ppermute | solution.py:27
  306.3 4.4 %collective-permute-done.20 = f32[1,256]{1,0:T(1,128)S(1)} collective-permute-done((f32[1,256]{1,0:T(1,128)S(1)}, f32[1,256]{1,0:T(1,128)S(1)}, u32[]{:S(2)}, u32[]{:S(2)}) %collective-permute-start.20) | collective-permute-done | bytes 1056 | tf_op jit(solution)/shard_map/ppermute | solution.py:27
  311.4 1.0 maximum_select_fusion.7
  (94 shorter events, 7.3 us)
Async XLA Ops:
  0.6 134.7 %copy-start = (bf16[1,64,16,1024]{3,2,1,0:T(8,128)(2,1)S(1)}, bf16[1,64,16,1024]{3,2,1,0:T(8,128)(2,1)}, u32[]{:S(2)}) copy-start(bf16[1,64,16,1024]{3,2,1,0:T(8,128)(2,1)} %param.6) | copy-start | bytes 6291460
  2.1 10.5 %collective-permute-start = (bf16[64,1024]{1,0:T(8,128)(2,1)S(1)}, bf16[64,1024]{1,0:T(8,128)(2,1)S(1)}, u32[]{:S(2)}, u32[]{:S(2)}) collective-permute-start(bf16[64,1024]{1,0:T(8,128)(2,1)S(1)} %bitcast.131), channel_id=1, source_target_pairs={{0,8},{1,9},{2,10},{3,11},{4,12},{5,13},{6,14},{7,15},{8,0},{9,1},... | collective-permute-start | bytes 393224 | tf_op jit(solution)/shard_map/ppermute | solution.py:27
  6.2 7.1 %collective-permute-start.4 = (bf16[64,1024]{1,0:T(8,128)(2,1)S(1)}, bf16[64,1024]{1,0:T(8,128)(2,1)S(1)}, u32[]{:S(2)}, u32[]{:S(2)}) collective-permute-start(bf16[64,1024]{1,0:T(8,128)(2,1)S(1)} %bitcast.144), channel_id=1, source_target_pairs={{0,4},{1,5},{2,6},{3,7},{4,0},{5,1},{6,2},{7,3},{8,12},{9,13},{10,... | collective-permute-start | bytes 393224 | tf_op jit(solution)/shard_map/ppermute | solution.py:27
  12.6 12.5 %collective-permute-start.1 = (bf16[2,64,1024]{2,1,0:T(8,128)(2,1)S(1)}, bf16[2,64,1024]{2,1,0:T(8,128)(2,1)S(1)}, u32[]{:S(2)}, u32[]{:S(2)}) collective-permute-start(bf16[2,64,1024]{2,1,0:T(8,128)(2,1)S(1)} %maximum_select_fusion.13), channel_id=1, source_target_pairs={{0,4},{1,5},{2,6},{3,7},{4,0},{5,1},{6,2},{7,3},{8,12},{9,13},{10,... | collective-permute-start | bytes 786440 | tf_op jit(solution)/shard_map/ppermute | solution.py:27
  13.3 15.3 %collective-permute-start.5 = (bf16[2,64,1024]{2,1,0:T(8,128)(2,1)S(1)}, bf16[2,64,1024]{2,1,0:T(8,128)(2,1)S(1)}, u32[]{:S(2)}, u32[]{:S(2)}) collective-permute-start(bf16[2,64,1024]{2,1,0:T(8,128)(2,1)S(1)} %maximum_select_fusion.15), channel_id=1, source_target_pairs={{0,8},{1,9},{2,10},{3,11},{4,12},{5,13},{6,14},{7,15},{8,0},{9,1},... | collective-permute-start | bytes 786440 | tf_op jit(solution)/shard_map/ppermute | solution.py:27
  25.3 11.5 %collective-permute-start.2 = (bf16[2,2,64,1024]{3,2,1,0:T(8,128)(2,1)S(1)}, bf16[2,2,64,1024]{3,2,1,0:T(8,128)(2,1)S(1)}, u32[]{:S(2)}, u32[]{:S(2)}) collective-permute-start(bf16[2,2,64,1024]{3,2,1,0:T(8,128)(2,1)S(1)} %maximum_select_fusion.9), channel_id=1, source_target_pairs={{0,2},{1,3},{2,0},{3,1},{4,6},{5,7},{6,4},{7,5},{8,10},{9,11},{10,... | collective-permute-start | bytes 1572872 | tf_op jit(solution)/shard_map/ppermute | solution.py:27
  28.7 10.8 %collective-permute-start.6 = (bf16[2,2,64,1024]{3,2,1,0:T(8,128)(2,1)S(1)}, bf16[2,2,64,1024]{3,2,1,0:T(8,128)(2,1)S(1)}, u32[]{:S(2)}, u32[]{:S(2)}) collective-permute-start(bf16[2,2,64,1024]{3,2,1,0:T(8,128)(2,1)S(1)} %maximum_select_fusion.11), channel_id=1, source_target_pairs={{0,1},{1,0},{2,3},{3,2},{4,5},{5,4},{6,7},{7,6},{8,9},{9,8},{10,11... | collective-permute-start | bytes 1572872 | tf_op jit(solution)/shard_map/ppermute | solution.py:27
  37.0 23.5 %collective-permute-start.3 = (bf16[2,2,2,64,1024]{4,3,1,0,2:T(8,128)(2,1)S(1)}, bf16[2,2,2,64,1024]{4,3,1,0,2:T(8,128)(2,1)S(1)}, u32[]{:S(2)}, u32[]{:S(2)}) collective-permute-start(bf16[2,2,2,64,1024]{4,3,1,0,2:T(8,128)(2,1)S(1)} %maximum_select_fusion.4), channel_id=1, source_target_pairs={{0,1},{1,0},{2,3},{3,2},{4,5},{5,4},{6,7},{7,6},{8,9},{9,8},{10,11... | collective-permute-start | bytes 3145736 | tf_op jit(solution)/shard_map/ppermute | solution.py:27
  39.7 21.3 %collective-permute-start.7 = (bf16[2,2,2,64,1024]{4,3,1,0,2:T(8,128)(2,1)S(1)}, bf16[2,2,2,64,1024]{4,3,1,0,2:T(8,128)(2,1)S(1)}, u32[]{:S(2)}, u32[]{:S(2)}) collective-permute-start(bf16[2,2,2,64,1024]{4,3,1,0,2:T(8,128)(2,1)S(1)} %maximum_select_fusion.6), channel_id=1, source_target_pairs={{0,2},{1,3},{2,0},{3,1},{4,6},{5,7},{6,4},{7,5},{8,10},{9,11},{10,... | collective-permute-start | bytes 3145736 | tf_op jit(solution)/shard_map/ppermute | solution.py:27
  61.6 3.6 %copy-start.2 = (bf16[1,64,64,256]{3,2,1,0:T(8,128)(2,1)S(1)}, bf16[1,64,64,256]{3,2,1,0:T(8,128)(2,1)}, u32[]{:S(2)}) copy-start(bf16[1,64,64,256]{3,2,1,0:T(8,128)(2,1)} %param.7) | copy-start | bytes 6291460
  65.2 51.3 %collective-permute-start.8 = (bf16[16,2,64,1024]{3,2,0,1:T(8,128)(2,1)}, bf16[16,2,64,1024]{3,2,0,1:T(8,128)(2,1)}, u32[]{:S(2)}, u32[]{:S(2)}) collective-permute-start(bf16[16,2,64,1024]{3,2,0,1:T(8,128)(2,1)} %get-tuple-element.9), channel_id=1, source_target_pairs={{0,16},{16,0},{1,17},{17,1},{2,18},{18,2},{3,19},{19,3},{4,20},{20... | collective-permute-start | bytes 12582920 | tf_op jit(solution)/shard_map/ppermute | solution.py:27
  66.6 14.9 %collective-permute-start.9 = (bf16[1024,256]{1,0:T(8,128)(2,1)}, bf16[1024,256]{1,0:T(8,128)(2,1)S(1)}, u32[]{:S(2)}, u32[]{:S(2)}) collective-permute-start(bf16[1024,256]{1,0:T(8,128)(2,1)} %bitcast.36), channel_id=1, source_target_pairs={{0,1},{1,0},{2,3},{3,2},{4,5},{5,4},{6,7},{7,6},{8,9},{9,8},{10,11... | collective-permute-start | bytes 1572872 | tf_op jit(solution)/shard_map/ppermute | solution.py:20
  68.1 24.7 %collective-permute-start.10 = (bf16[1024,256]{1,0:T(8,128)(2,1)}, bf16[1024,256]{1,0:T(8,128)(2,1)S(1)}, u32[]{:S(2)}, u32[]{:S(2)}) collective-permute-start(bf16[1024,256]{1,0:T(8,128)(2,1)} %bitcast.37), channel_id=1, source_target_pairs={{0,1},{1,0},{2,3},{3,2},{4,5},{5,4},{6,7},{7,6},{8,9},{9,8},{10,11... | collective-permute-start | bytes 1572872 | tf_op jit(solution)/shard_map/ppermute | solution.py:20
  68.6 35.5 %collective-permute-start.11 = (bf16[1024,256]{1,0:T(8,128)(2,1)}, bf16[1024,256]{1,0:T(8,128)(2,1)}, u32[]{:S(2)}, u32[]{:S(2)}) collective-permute-start(bf16[1024,256]{1,0:T(8,128)(2,1)} %bitcast.38), channel_id=1, source_target_pairs={{0,1},{1,0},{2,3},{3,2},{4,5},{5,4},{6,7},{7,6},{8,9},{9,8},{10,11... | collective-permute-start | bytes 1572872 | tf_op jit(solution)/shard_map/ppermute | solution.py:20
  70.1 44.8 %collective-permute-start.12 = (bf16[1024,256]{1,0:T(8,128)(2,1)}, bf16[1024,256]{1,0:T(8,128)(2,1)}, u32[]{:S(2)}, u32[]{:S(2)}) collective-permute-start(bf16[1024,256]{1,0:T(8,128)(2,1)} %bitcast.39), channel_id=1, source_target_pairs={{0,1},{1,0},{2,3},{3,2},{4,5},{5,4},{6,7},{7,6},{8,9},{9,8},{10,11... | collective-permute-start | bytes 1572872 | tf_op jit(solution)/shard_map/ppermute | solution.py:20
  70.7 4.1 %copy-start.15 = (s32[1,64,16]{1,2,0:T(8,128)S(1)}, s32[1,64,16]{1,2,0:T(8,128)}, u32[]{:S(2)}) copy-start(s32[1,64,16]{1,2,0:T(8,128)} %param.8) | copy-start | bytes 12292
  81.5 68.4 %collective-permute-start.13 = (bf16[1024,256]{1,0:T(8,128)(2,1)S(1)}, bf16[1024,256]{1,0:T(8,128)(2,1)S(1)}, u32[]{:S(2)}, u32[]{:S(2)}) collective-permute-start(bf16[1024,256]{1,0:T(8,128)(2,1)S(1)} %collective-permute-done.9.rest_0_), channel_id=1, source_target_pairs={{0,2},{1,15},{2,4},{3,1},{4,6},{5,3},{6,8},{7,5},{8,10},{9,7},{10,... | collective-permute-start | bytes 1572872 | tf_op jit(solution)/shard_map/ppermute | solution.py:21
  92.8 57.1 %collective-permute-start.14 = (bf16[1024,256]{1,0:T(8,128)(2,1)S(1)}, bf16[1024,256]{1,0:T(8,128)(2,1)S(1)}, u32[]{:S(2)}, u32[]{:S(2)}) collective-permute-start(bf16[1024,256]{1,0:T(8,128)(2,1)S(1)} %collective-permute-done.10.rest_1_), channel_id=1, source_target_pairs={{0,2},{1,15},{2,4},{3,1},{4,6},{5,3},{6,8},{7,5},{8,10},{9,7},{10,... | collective-permute-start | bytes 1572872 | tf_op jit(solution)/shard_map/ppermute | solution.py:21
  104.1 45.8 %collective-permute-start.15 = (bf16[1024,256]{1,0:T(8,128)(2,1)}, bf16[1024,256]{1,0:T(8,128)(2,1)S(1)}, u32[]{:S(2)}, u32[]{:S(2)}) collective-permute-start(bf16[1024,256]{1,0:T(8,128)(2,1)} %collective-permute-done.11.rest_2_), channel_id=1, source_target_pairs={{0,2},{1,15},{2,4},{3,1},{4,6},{5,3},{6,8},{7,5},{8,10},{9,7},{10,... | collective-permute-start | bytes 1572872 | tf_op jit(solution)/shard_map/ppermute | solution.py:21
  115.0 34.9 %collective-permute-start.16 = (bf16[1024,256]{1,0:T(8,128)(2,1)}, bf16[1024,256]{1,0:T(8,128)(2,1)S(1)}, u32[]{:S(2)}, u32[]{:S(2)}) collective-permute-start(bf16[1024,256]{1,0:T(8,128)(2,1)} %collective-permute-done.12.rest_3_), channel_id=1, source_target_pairs={{0,2},{1,15},{2,4},{3,1},{4,6},{5,3},{6,8},{7,5},{8,10},{9,7},{10,... | collective-permute-start | bytes 1572872 | tf_op jit(solution)/shard_map/ppermute | solution.py:21
  135.3 14.6 %copy-start.3 = (bf16[1,64,64,256]{3,2,1,0:T(8,128)(2,1)S(1)}, bf16[1,64,64,256]{3,2,1,0:T(8,128)(2,1)}, u32[]{:S(2)}) copy-start(bf16[1,64,64,256]{3,2,1,0:T(8,128)(2,1)} %param.7) | copy-start | bytes 6291460
  135.3 14.6 %copy-start.4 = (bf16[64,32,2,256]{3,1,2,0:T(8,128)(2,1)S(1)}, bf16[64,32,2,256]{3,1,2,0:T(8,128)(2,1)}, u32[]{:S(2)}) copy-start(bf16[64,32,2,256]{3,1,2,0:T(8,128)(2,1)} %copy.32) | copy-start | bytes 6291460
  135.3 14.6 %copy-start.5 = (f32[1,256]{1,0:T(1,128)S(1)}, f32[1,256]{1,0:T(1,128)}, u32[]{:S(2)}) copy-start(f32[1,256]{1,0:T(1,128)} %occ_ref.1) | copy-start | bytes 3076
  135.3 14.6 %copy-start.6 = (s32[1,64]{1,0:T(1,128)S(1)}, s32[1,64]{1,0:T(1,128)}, u32[]{:S(2)}) copy-start(s32[1,64]{1,0:T(1,128)} %param.9) | copy-start | bytes 772
  200.5 2.6 copy-start.7
  200.6 3.9 %copy-start.9 = (bf16[16,2,1,64,1024]{4,3,2,1,0:T(8,128)(2,1)}, bf16[16,2,1,64,1024]{4,3,2,1,0:T(8,128)(2,1)S(1)}, u32[]{:S(2)}) copy-start(bf16[16,2,1,64,1024]{4,3,2,1,0:T(8,128)(2,1)S(1)} %get-tuple-element.6) | copy-start | bytes 12582916
  202.3 4.5 %collective-permute-start.21 = (bf16[16,64,1024]{2,1,0:T(8,128)(2,1)}, bf16[16,64,1024]{2,1,0:T(8,128)(2,1)}, u32[]{:S(2)}, u32[]{:S(2)}) collective-permute-start(bf16[16,64,1024]{2,1,0:T(8,128)(2,1)} %dynamic-slice_bitcast_fusion.1), channel_id=1, source_target_pairs={{0,16},{16,0},{1,17},{17,1},{2,18},{18,2},{3,19},{19,3},{4,20},{20... | collective-permute-start | bytes 6291464 | tf_op jit(solution)/shard_map/ppermute | solution.py:27
  204.5 13.5 %collective-permute-start.26 = (bf16[16,64,1024]{2,1,0:T(8,128)(2,1)S(1)}, bf16[16,64,1024]{2,1,0:T(8,128)(2,1)}, u32[]{:S(2)}, u32[]{:S(2)}) collective-permute-start(bf16[16,64,1024]{2,1,0:T(8,128)(2,1)S(1)} %dynamic-slice_bitcast_fusion), channel_id=1, source_target_pairs={{0,16},{16,0},{1,17},{17,1},{2,18},{18,2},{3,19},{19,3},{4,20},{20... | collective-permute-start | bytes 6291464 | tf_op jit(solution)/shard_map/ppermute | solution.py:27
  206.8 11.2 %copy-start.8 = (bf16[16,2,1,64,1024]{4,3,2,1,0:T(8,128)(2,1)S(1)}, bf16[16,2,1,64,1024]{4,3,2,1,0:T(8,128)(2,1)}, u32[]{:S(2)}) copy-start(bf16[16,2,1,64,1024]{4,3,2,1,0:T(8,128)(2,1)} %copy-done.7) | copy-start | bytes 12582916
  210.1 7.9 %copy-start.12 = (f32[16,64,1024]{2,1,0:T(8,128)}, f32[16,64,1024]{2,1,0:T(8,128)S(1)}, u32[]{:S(2)}) copy-start(f32[16,64,1024]{2,1,0:T(8,128)S(1)} %convert_add_fusion.1) | copy-start | bytes 12582916
  210.3 31.2 %collective-permute-start.22 = (bf16[2,2,2,64,1024]{4,3,2,1,0:T(8,128)(2,1)S(1)}, bf16[2,2,2,64,1024]{4,3,2,1,0:T(8,128)(2,1)}, u32[]{:S(2)}, u32[]{:S(2)}) collective-permute-start(bf16[2,2,2,64,1024]{4,3,2,1,0:T(8,128)(2,1)S(1)} %fusion), channel_id=1, source_target_pairs={{0,1},{1,0},{2,3},{3,2},{4,5},{5,4},{6,7},{7,6},{8,9},{9,8},{10,11... | collective-permute-start | bytes 3145736 | tf_op jit(solution)/shard_map/ppermute | solution.py:27
  220.5 2.0 copy-start.10
  223.6 26.4 %collective-permute-start.27 = (bf16[2,2,2,64,1024]{4,3,2,1,0:T(8,128)(2,1)}, bf16[2,2,2,64,1024]{4,3,2,1,0:T(8,128)(2,1)}, u32[]{:S(2)}, u32[]{:S(2)}) collective-permute-start(bf16[2,2,2,64,1024]{4,3,2,1,0:T(8,128)(2,1)} %fusion.1), channel_id=1, source_target_pairs={{0,2},{1,3},{2,0},{3,1},{4,6},{5,7},{6,4},{7,5},{8,10},{9,11},{10,... | collective-permute-start | bytes 3145736 | tf_op jit(solution)/shard_map/ppermute | solution.py:27
  223.6 26.4 %copy-start.11 = (f32[16,64,1024]{2,1,0:T(8,128)S(1)}, f32[16,64,1024]{2,1,0:T(8,128)}, u32[]{:S(2)}) copy-start(f32[16,64,1024]{2,1,0:T(8,128)} %copy-done.10) | copy-start | bytes 12582916
  244.0 16.1 %collective-permute-start.23 = (bf16[2,2,64,1024]{3,2,1,0:T(8,128)(2,1)S(1)}, bf16[2,2,64,1024]{3,2,1,0:T(8,128)(2,1)}, u32[]{:S(2)}, u32[]{:S(2)}) collective-permute-start(bf16[2,2,64,1024]{3,2,1,0:T(8,128)(2,1)S(1)} %fusion.2), channel_id=1, source_target_pairs={{0,2},{1,3},{2,0},{3,1},{4,6},{5,7},{6,4},{7,5},{8,10},{9,11},{10,... | collective-permute-start | bytes 1572872 | tf_op jit(solution)/shard_map/ppermute | solution.py:27
  251.7 1.3 copy-start.13
  253.1 12.5 %collective-permute-start.28 = (bf16[2,2,64,1024]{3,2,1,0:T(8,128)(2,1)S(1)}, bf16[2,2,64,1024]{3,2,1,0:T(8,128)(2,1)}, u32[]{:S(2)}, u32[]{:S(2)}) collective-permute-start(bf16[2,2,64,1024]{3,2,1,0:T(8,128)(2,1)S(1)} %fusion.3), channel_id=1, source_target_pairs={{0,1},{1,0},{2,3},{3,2},{4,5},{5,4},{6,7},{7,6},{8,9},{9,8},{10,11... | collective-permute-start | bytes 1572872 | tf_op jit(solution)/shard_map/ppermute | solution.py:27
  254.9 10.7 %copy-start.14 = (f32[2,2,2,64,1024]{4,3,2,1,0:T(8,128)S(1)}, f32[2,2,2,64,1024]{4,3,2,1,0:T(8,128)}, u32[]{:S(2)}) copy-start(f32[2,2,2,64,1024]{4,3,2,1,0:T(8,128)} %copy-done.13) | copy-start | bytes 6291460
  261.3 7.9 %collective-permute-start.24 = (bf16[2,64,1024]{2,1,0:T(8,128)(2,1)S(1)}, bf16[2,64,1024]{2,1,0:T(8,128)(2,1)S(1)}, u32[]{:S(2)}, u32[]{:S(2)}) collective-permute-start(bf16[2,64,1024]{2,1,0:T(8,128)(2,1)S(1)} %fusion.4), channel_id=1, source_target_pairs={{0,4},{1,5},{2,6},{3,7},{4,0},{5,1},{6,2},{7,3},{8,12},{9,13},{10,... | collective-permute-start | bytes 786440 | tf_op jit(solution)/shard_map/ppermute | solution.py:27
  266.8 18.5 %collective-permute-start.29 = (bf16[2,64,1024]{2,1,0:T(8,128)(2,1)S(1)}, bf16[2,64,1024]{2,1,0:T(8,128)(2,1)S(1)}, u32[]{:S(2)}, u32[]{:S(2)}) collective-permute-start(bf16[2,64,1024]{2,1,0:T(8,128)(2,1)S(1)} %fusion.5), channel_id=1, source_target_pairs={{0,8},{1,9},{2,10},{3,11},{4,12},{5,13},{6,14},{7,15},{8,0},{9,1},... | collective-permute-start | bytes 786440 | tf_op jit(solution)/shard_map/ppermute | solution.py:27
  269.4 20.5 %collective-permute-start.25 = (f32[64,1024]{1,0:T(8,128)S(1)}, f32[64,1024]{1,0:T(8,128)S(1)}, u32[]{:S(2)}, u32[]{:S(2)}) collective-permute-start(f32[64,1024]{1,0:T(8,128)S(1)} %dynamic-slice_bitcast_fusion.3), channel_id=1, source_target_pairs={{0,8},{1,9},{2,10},{3,11},{4,12},{5,13},{6,14},{7,15},{8,0},{9,1},... | collective-permute-start | bytes 786440 | tf_op jit(solution)/shard_map/ppermute | solution.py:27
  285.4 10.0 %collective-permute-start.30 = (f32[64,1024]{1,0:T(8,128)S(1)}, f32[64,1024]{1,0:T(8,128)S(1)}, u32[]{:S(2)}, u32[]{:S(2)}) collective-permute-start(f32[64,1024]{1,0:T(8,128)S(1)} %dynamic-slice_bitcast_fusion.2), channel_id=1, source_target_pairs={{0,4},{1,5},{2,6},{3,7},{4,0},{5,1},{6,2},{7,3},{8,12},{9,13},{10,... | collective-permute-start | bytes 786440 | tf_op jit(solution)/shard_map/ppermute | solution.py:27
  289.8 22.6 %copy-start.1 = (bf16[1,64,16,1024]{3,2,1,0:T(8,128)(2,1)S(1)}, bf16[1,64,16,1024]{3,2,1,0:T(8,128)(2,1)}, u32[]{:S(2)}) copy-start(bf16[1,64,16,1024]{3,2,1,0:T(8,128)(2,1)} %param.6) | copy-start | bytes 6291460
  295.5 15.9 %collective-permute-start.31 = (f32[2,64,1024]{2,1,0:T(8,128)S(1)}, f32[2,64,1024]{2,1,0:T(8,128)S(1)}, u32[]{:S(2)}, u32[]{:S(2)}) collective-permute-start(f32[2,64,1024]{2,1,0:T(8,128)S(1)} %get-tuple-element.15), channel_id=1, source_target_pairs={{0,16},{16,0},{1,17},{17,1},{2,18},{18,2},{3,19},{19,3},{4,20},{20... | collective-permute-start | bytes 1572872 | tf_op jit(solution)/shard_map/ppermute | solution.py:27
  295.5 3.6 %collective-permute-start.17 = (f32[1,256]{1,0:T(1,128)S(1)}, f32[1,256]{1,0:T(1,128)S(1)}, u32[]{:S(2)}, u32[]{:S(2)}) collective-permute-start(f32[1,256]{1,0:T(1,128)S(1)} %get-tuple-element.4), channel_id=1, source_target_pairs={{0,1},{1,0},{2,3},{3,2},{4,5},{5,4},{6,7},{7,6},{8,9},{9,8},{10,11... | collective-permute-start | bytes 3080 | tf_op jit(solution)/shard_map/ppermute | solution.py:27
  299.2 3.6 %collective-permute-start.18 = (f32[1,256]{1,0:T(1,128)S(1)}, f32[1,256]{1,0:T(1,128)S(1)}, u32[]{:S(2)}, u32[]{:S(2)}) collective-permute-start(f32[1,256]{1,0:T(1,128)S(1)} %add.131), channel_id=1, source_target_pairs={{0,2},{1,3},{2,0},{3,1},{4,6},{5,7},{6,4},{7,5},{8,10},{9,11},{10,... | collective-permute-start | bytes 3080 | tf_op jit(solution)/shard_map/ppermute | solution.py:27
  302.8 3.6 %collective-permute-start.19 = (f32[1,256]{1,0:T(1,128)S(1)}, f32[1,256]{1,0:T(1,128)S(1)}, u32[]{:S(2)}, u32[]{:S(2)}) collective-permute-start(f32[1,256]{1,0:T(1,128)S(1)} %add.132), channel_id=1, source_target_pairs={{0,4},{1,5},{2,6},{3,7},{4,0},{5,1},{6,2},{7,3},{8,12},{9,13},{10,... | collective-permute-start | bytes 3080 | tf_op jit(solution)/shard_map/ppermute | solution.py:27
  306.3 4.5 %collective-permute-start.20 = (f32[1,256]{1,0:T(1,128)S(1)}, f32[1,256]{1,0:T(1,128)S(1)}, u32[]{:S(2)}, u32[]{:S(2)}) collective-permute-start(f32[1,256]{1,0:T(1,128)S(1)} %add.133), channel_id=1, source_target_pairs={{0,8},{1,9},{2,10},{3,11},{4,12},{5,13},{6,14},{7,15},{8,0},{9,1},... | collective-permute-start | bytes 3080 | tf_op jit(solution)/shard_map/ppermute | solution.py:27
